TPU v7x, 512 devices: a whole 4x4x16 slice. The times are simulated.
512 devices in a mesh: wide: 128 (over z, y, core), narrow: 4 (over x).
Axes of the slice: x: 4, y: 4, z: 16, core: 2. Of those that a mesh axis runs over, the one named last changes fastest.
Arguments:
- pressure_head: float32 [64, 512, 1024], P('narrow', 'wide'), may hold values from -3 to 0.5
- texture: int32 [64, 512, 1024], P('narrow', 'wide'), may hold values from 0 to 11
- saturated_table: float32 [12], replicated, may hold values from 0.1 to 1
- shape_table: float32 [12], replicated, may hold values from 0.3 to 3
- capacity_table: float32 [12], replicated, may hold values from 0.5 to 2
- uptake: float32 [32768, 64], P('wide', 'narrow'), may hold values from 0.02 to 0.5
- root_tile: int32 [32768, 1], P('wide'), may hold values from 0 to 127; in each aligned block of 256 rows (0 to 255, 256 to 511, ...) at most 4 rows name the same one
- root_column: int32 [32768], P('wide'), may hold values from 0 to 4095
- aquifer_head: float32 [3, 512, 1024], P(None, 'wide'), may hold values from -4 to 4
- transmissivity: float32 [3, 512, 1024], P(None, 'wide'), may hold values from 0.5 to 5
Outputs:
- head_next: float32 [64, 512, 1024], P('narrow', 'wide')
- aquifer_next: float32 [3, 512, 1024], P(None, 'wide', 'narrow')
Inputs may be any that keep to these rules, and one draw needn't show every extreme that they name: `root_tile`: within each aligned block of 256 rows no tile is named more than 4 times, a bound that some block reaches.
All inputs are finite; a program needn't handle non-finite values.
Results may differ from a plain program's by a relative error of at most 0.0003.
Values sent between devices are 32-bit elements; how exact they have to be, the bound alone decides.
A program may use at most 128 MiB of HBM per device.

v0:
```python
import jax
import jax.numpy as jnp
from jax import lax
from jax.sharding import PartitionSpec as P

SWEEPS = 8


TIME_STEP = 0.25
STORAGE = 0.05
LEAKANCE = 0.5


def padded_2(cells, sides, width):
    for axis, dim in sides:
        count = lax.axis_size(axis)
        ends = count - 1
        head = lax.slice_in_dim(cells, 0, width, axis=dim)
        tail = lax.slice_in_dim(cells, cells.shape[dim] - width, cells.shape[dim], axis=dim)
        cells = jnp.concatenate(
            [
                lax.ppermute(tail, axis, [(i, (i + 1) % count) for i in range(ends)]),
                cells,
                lax.ppermute(head, axis, [((i + 1) % count, i) for i in range(ends)]),
            ],
            axis=dim,
        )
    return cells


def broadcast(block, axis, source):
    block = jnp.where(lax.axis_index(axis) == source, block, jnp.zeros_like(block))
    return lax.psum(block, axis)


def texture_values(texture, saturated_table, shape_table, capacity_table):
    tables = (saturated_table, shape_table, capacity_table)
    zero_field = jnp.zeros(texture.shape, saturated_table.dtype)

    def pick(class_index, carried):
        matched = texture == class_index
        return tuple(
            (
                jnp.where(matched, table[class_index], current)
                for table, current in zip(tables, carried)
            )
        )

    return lax.fori_loop(0, saturated_table.shape[0], pick, (zero_field, zero_field, zero_field))


def relax(heads, fixed):
    previous = fixed[0:3, 1:-1, 1:-1]
    transmit = fixed[3:6]
    recharge = fixed[6, 1:-1, 1:-1]
    inside = fixed[7, 1:-1, 1:-1]
    centre_trans = transmit[:, 1:-1, 1:-1]
    north_face = 0.5 * (centre_trans + transmit[:, :-2, 1:-1])
    south_face = 0.5 * (centre_trans + transmit[:, 2:, 1:-1])
    west_face = 0.5 * (centre_trans + transmit[:, 1:-1, :-2])
    east_face = 0.5 * (centre_trans + transmit[:, 1:-1, 2:])
    inflow = (
        north_face * heads[:, :-2, 1:-1]
        + south_face * heads[:, 2:, 1:-1]
        + west_face * heads[:, 1:-1, :-2]
        + east_face * heads[:, 1:-1, 2:]
    )
    centre = heads[:, 1:-1, 1:-1]
    blank_layer = jnp.zeros_like(centre[:1])
    upward = jnp.concatenate([blank_layer, centre[:-1]], axis=0)
    downward = jnp.concatenate([centre[1:], blank_layer], axis=0)
    single = jnp.ones_like(blank_layer)
    link_count = jnp.concatenate([single, 2.0 * single, single], axis=0)
    top_source = jnp.concatenate([recharge[None], jnp.zeros_like(centre[1:])], axis=0)
    source = STORAGE * previous + inflow + LEAKANCE * (upward + downward) + top_source
    divisor = STORAGE + north_face + south_face + west_face + east_face + LEAKANCE * link_count
    return source / divisor * inside


def widen_static(values, spread):
    rows = padded_2(values, (("wide", 1),), spread)
    return jnp.pad(rows, ((0, 0), (0, 0), (spread, spread)))


def widen_heads(values, spread):
    rows = padded_2(values, (("wide", 1),), spread)
    return jnp.pad(rows, ((0, 0), (0, 0), (spread, spread)))


def body(
    pressure_head,
    texture,
    saturated_table,
    shape_table,
    capacity_table,
    uptake,
    root_tile,
    root_column,
    aquifer_head,
    transmissivity,
):
    layer_count, row_count, col_count = pressure_head.shape
    wide_count = lax.axis_size("wide")
    narrow_count = lax.axis_size("narrow")
    saturated, shape_rate, capacity = texture_values(
        texture, saturated_table, shape_table, capacity_table
    )
    conduct = saturated * jnp.exp(shape_rate * jnp.minimum(pressure_head, 0.0))
    padded = padded_2(jnp.stack([pressure_head, conduct]), (("wide", 2), ("narrow", 1)), 1)
    root_count = uptake.shape[0]
    tile_ids = root_tile[:, 0]
    slot_count = max(2, 2 * root_count // wide_count)
    every_uptake, every_tile, every_column = (
        lax.all_gather(uptake, "wide", axis=0, tiled=True),
        lax.all_gather(tile_ids, "wide", axis=0, tiled=True),
        lax.all_gather(root_column, "wide", axis=0, tiled=True),
    )
    matched = (
        (every_tile == lax.axis_index("wide")).reshape(wide_count, root_count).astype(jnp.int32)
    )
    block_rank = jnp.cumsum(matched, axis=1) - 1
    block_base = (jnp.arange(wide_count, dtype=jnp.int32) * slot_count)[:, None]
    slot_total = wide_count * slot_count
    slot_index = jnp.where(matched > 0, block_base + block_rank, slot_total).reshape(-1)
    row_numbers = jnp.arange(wide_count * root_count, dtype=jnp.int32) + 1
    picked = jnp.zeros((slot_total + 1,), jnp.int32).at[slot_index].set(row_numbers)[:slot_total]
    uptake_rows = jnp.concatenate([jnp.zeros((1, layer_count), jnp.float32), every_uptake], axis=0)
    column_rows = jnp.concatenate([jnp.zeros((1,), jnp.int32), every_column], axis=0)
    amounts = jnp.take(uptake_rows, picked, axis=0)
    places = jnp.take(column_rows, picked, axis=0)
    uptake_sum = (
        jnp.zeros((layer_count, row_count * col_count), jnp.float32)
        .at[:, places]
        .add(amounts.T)
        .reshape(layer_count, row_count, col_count)
    )
    top_slab = lax.axis_index("narrow") == 0
    bottom_slab = lax.axis_index("narrow") == narrow_count - 1
    first_tile = lax.axis_index("wide") == 0
    last_tile = lax.axis_index("wide") == wide_count - 1
    head_pad = padded[0]
    cond_pad = padded[1]
    drainage = conduct[-1] * (pressure_head[-1] - aquifer_head[0] + 1.0)
    vertical = (
        0.5
        * (cond_pad[:-1, 1:-1] + cond_pad[1:, 1:-1])
        * (head_pad[:-1, 1:-1] - head_pad[1:, 1:-1] + 1.0)
    )
    vertical = jnp.concatenate(
        [
            jnp.where(top_slab, 0.0, vertical[:1]),
            vertical[1:-1],
            jnp.where(bottom_slab, drainage[None], vertical[-1:]),
        ],
        axis=0,
    )
    across = (
        0.5
        * (cond_pad[1:-1, :-1] + cond_pad[1:-1, 1:])
        * (head_pad[1:-1, :-1] - head_pad[1:-1, 1:])
    )
    across = jnp.concatenate(
        [
            jnp.where(first_tile, 0.0, across[:, :1]),
            across[:, 1:-1],
            jnp.where(last_tile, 0.0, across[:, -1:]),
        ],
        axis=1,
    )
    along = (
        0.5
        * (conduct[:, :, :-1] + conduct[:, :, 1:])
        * (pressure_head[:, :, :-1] - pressure_head[:, :, 1:])
    )
    edge_zeros = jnp.zeros_like(along[:, :, :1])
    along = jnp.concatenate([edge_zeros, along, edge_zeros], axis=2)
    balance = (
        vertical[:-1]
        - vertical[1:]
        + (across[:, :-1] - across[:, 1:])
        + (along[:, :, :-1] - along[:, :, 1:])
        - uptake_sum
    )
    head_next = pressure_head + TIME_STEP * balance / capacity
    drainage_all = broadcast(drainage, "narrow", narrow_count - 1)
    quarter = col_count // narrow_count
    start = lax.axis_index("narrow") * quarter
    spread = 1
    fixed = jnp.concatenate(
        [aquifer_head, transmissivity, drainage_all[None], jnp.ones_like(drainage_all)[None]],
        axis=0,
    )
    fixed = widen_static(fixed, spread)
    heads = aquifer_head
    for rounds in range(SWEEPS // spread):
        current = widen_heads(heads, spread)
        current = relax(current, fixed)
        heads = current
    aquifer_next = lax.dynamic_slice_in_dim(heads, start, quarter, 2)
    return (head_next, aquifer_next)


def solution(mesh):
    in_specs = (
        P("narrow", "wide", None),
        P("narrow", "wide", None),
        P(),
        P(),
        P(),
        P("wide", "narrow"),
        P("wide", None),
        P("wide"),
        P(None, "wide", None),
        P(None, "wide", None),
    )
    out_specs = (P("narrow", "wide", None), P(None, "wide", "narrow"))
    return jax.shard_map(body, mesh=mesh, in_specs=in_specs, out_specs=out_specs, check_vma=False)
```

profile of v0, /device:TPU:121, one launch (start us, length us, event | category | flops | bytes accessed | tf_op | source)
XLA Modules:
  0.0 553.6 jit_solution(12828697099935549018)
XLA Ops:
  8.1 5.0 collective-permute-start.5
  13.1 1.9 collective-permute-start.7
  16.6 83.6 %while.18 = (s32[]{:T(128)}, f32[16,4,1024]{2,1,0:T(4,128)S(1)}, f32[16,4,1024]{2,1,0:T(4,128)S(1)}, f32[16,4,1024]{2,1,0:T(4,128)S(1)}, s32[16,4,1024]{2,1,0:T(...) while((s32[]{:T(128)}, f32[16,4,1024]{2,1,0:T(4,128)S(1)}, ...), condition=%wide.region_1.2_spmd.clone, body=%wide.region_0.1_spmd.clone.sunk | while | flops 458755 | bytes 1966252 | solution.py:49
  20.3 1.8 select_select_fusion.5
  27.3 1.8 select_select_fusion.5
  34.2 1.8 select_select_fusion.5
  41.2 1.8 select_select_fusion.5
  48.1 1.8 select_select_fusion.5
  55.1 1.8 select_select_fusion.5
  62.1 1.8 select_select_fusion.5
  69.0 1.8 select_select_fusion.5
  76.0 1.8 select_select_fusion.5
  83.0 1.8 select_select_fusion.5
  100.5 7.0 %collective-permute-start = (f32[2,16,1,1024]{3,2,1,0:T(1,128)S(1)}, f32[2,16,1,1024]{3,2,1,0:T(1,128)S(1)}, u32[]{:S(2)}, u32[]{:S(2)}) collective-permute-start(f32[2,16,1,1024]{3,2,1,0:T(1,128)S(1)} %get-tuple-element.210), channel_id=1, source_target_pairs={{0,4},{4,8},{8,12},{12,16},{16,20},{20,24},{24,28},{28,32},{32,36}... | collective-permute-start | bytes 393224 | tf_op jit(solution)/shard_map/ppermute | solution.py:22
  107.5 1.9 collective-permute-start.1
  110.7 84.4 %all-gather = s32[32768,1]{0,1:T(1,128)S(1)} all-gather(s32[256,1]{0,1:T(1,128)S(1)} %copy-done.9), channel_id=2, replica_groups=mesh['wide'=128,'narrow'=4] {'wide'}, dimensions={0}, use_global_device_ids=true | all-gather | bytes 132096 | tf_op jit(solution)/shard_map/all_gather | solution.py:115
  196.0 120.0 %scatter_custom_fusion = s32[513]{0:T(1024)S(1)} fusion(s32[32768]{0:T(1024)S(1)} %get-tuple-element.251, s32[32768]{0:T(1024)S(1)} %get-tuple-element.252, s32[]{:T(128)} %constant.37.clone.1), kind=kCustom, calls=%fused_computation.218 | custom fusion | bytes 2056 | tf_op jit(solution)/shard_map/scatter | solution.py:126
  316.1 82.4 %all-gather.1 = s32[128,1,256]{2,1,0:T(1,128)S(1)} all-gather(s32[1,1,256]{2,1,0:T(1,128)S(1)} %bitcast.38), channel_id=1, replica_groups=mesh['wide'=128,'narrow'=4] {'wide'}, dimensions={0}, use_global_device_ids=true | all-gather | bytes 132096 | tf_op jit(solution)/shard_map/all_gather | solution.py:116
  398.6 3.1 gather_fusion
  401.9 3.1 collective-permute-start.2
  406.5 3.5 collective-permute-done.3
  411.5 12.0 %psum.7 = f32[1,4,1024]{2,1,0:T(4,128)S(1)} all-reduce(f32[1,4,1024]{2,1,0:T(4,128)S(1)} %get-tuple-element.206), channel_id=1, replica_groups=mesh['wide'=128,'narrow'=4] {'narrow'}, use_global_device_ids=true, to_apply=%region_6.7 | all-reduce | flops 4096 | bytes 32768 | tf_op jit(solution)/shard_map/psum | solution.py:33
  423.6 7.1 %collective-permute-start.6 = (f32[8,1,1024]{2,1,0:T(1,128)S(1)}, f32[8,1,1024]{2,1,0:T(1,128)S(1)}, u32[]{:S(2)}, u32[]{:S(2)}) collective-permute-start(f32[8,1,1024]{2,1,0:T(1,128)S(1)} %get-tuple-element.213), channel_id=1, source_target_pairs={{4,0},{8,4},{12,8},{16,12},{20,16},{24,20},{28,24},{32,28},{36,32}... | collective-permute-start | bytes 98312 | tf_op jit(solution)/shard_map/ppermute | solution.py:24
  430.7 4.2 collective-permute-start.4
  437.0 7.0 %collective-permute-start.8 = (f32[3,1,1024]{2,1,0:T(1,128)S(1)}, f32[3,1,1024]{2,1,0:T(1,128)S(1)}, u32[]{:S(2)}, u32[]{:S(2)}) collective-permute-start(f32[3,1,1024]{2,1,0:T(1,128)S(1)} %get-tuple-element.245), channel_id=1, source_target_pairs={{0,4},{4,8},{8,12},{12,16},{16,20},{20,24},{24,28},{28,32},{32,36}... | collective-permute-start | bytes 36872 | tf_op jit(solution)/shard_map/ppermute | solution.py:22
  444.0 1.9 collective-permute-start.9
  446.0 6.4 %collective-permute-done.9 = f32[3,1,1024]{2,1,0:T(1,128)S(1)} collective-permute-done((f32[3,1,1024]{2,1,0:T(1,128)S(1)}, f32[3,1,1024]{2,1,0:T(1,128)S(1)}, u32[]{:S(2)}, u32[]{:S(2)}) %collective-permute-start.9) | collective-permute-done | bytes 12320 | tf_op jit(solution)/shard_map/ppermute | solution.py:24
  452.7 1.9 collective-permute-start.10
  454.6 2.4 collective-permute-start.11
  457.1 5.9 %collective-permute-done.11 = f32[3,1,1024]{2,1,0:T(1,128)S(1)} collective-permute-done((f32[3,1,1024]{2,1,0:T(1,128)S(1)}, f32[3,1,1024]{2,1,0:T(1,128)S(1)}, u32[]{:S(2)}, u32[]{:S(2)}) %collective-permute-start.11) | collective-permute-done | bytes 12320 | tf_op jit(solution)/shard_map/ppermute | solution.py:24
  463.3 1.9 collective-permute-start.12
  465.3 2.4 collective-permute-start.13
  467.7 5.9 %collective-permute-done.13 = f32[3,1,1024]{2,1,0:T(1,128)S(1)} collective-permute-done((f32[3,1,1024]{2,1,0:T(1,128)S(1)}, f32[3,1,1024]{2,1,0:T(1,128)S(1)}, u32[]{:S(2)}, u32[]{:S(2)}) %collective-permute-start.13) | collective-permute-done | bytes 12320 | tf_op jit(solution)/shard_map/ppermute | solution.py:24
  473.9 1.9 collective-permute-start.14
  475.9 2.4 collective-permute-start.15
  478.3 5.9 %collective-permute-done.15 = f32[3,1,1024]{2,1,0:T(1,128)S(1)} collective-permute-done((f32[3,1,1024]{2,1,0:T(1,128)S(1)}, f32[3,1,1024]{2,1,0:T(1,128)S(1)}, u32[]{:S(2)}, u32[]{:S(2)}) %collective-permute-start.15) | collective-permute-done | bytes 12320 | tf_op jit(solution)/shard_map/ppermute | solution.py:24
  484.5 1.9 collective-permute-start.16
  486.5 2.4 collective-permute-start.17
  488.9 5.9 %collective-permute-done.17 = f32[3,1,1024]{2,1,0:T(1,128)S(1)} collective-permute-done((f32[3,1,1024]{2,1,0:T(1,128)S(1)}, f32[3,1,1024]{2,1,0:T(1,128)S(1)}, u32[]{:S(2)}, u32[]{:S(2)}) %collective-permute-start.17) | collective-permute-done | bytes 12320 | tf_op jit(solution)/shard_map/ppermute | solution.py:24
  495.1 1.9 collective-permute-start.18
  497.1 2.4 collective-permute-start.19
  499.5 5.9 %collective-permute-done.19 = f32[3,1,1024]{2,1,0:T(1,128)S(1)} collective-permute-done((f32[3,1,1024]{2,1,0:T(1,128)S(1)}, f32[3,1,1024]{2,1,0:T(1,128)S(1)}, u32[]{:S(2)}, u32[]{:S(2)}) %collective-permute-start.19) | collective-permute-done | bytes 12320 | tf_op jit(solution)/shard_map/ppermute | solution.py:24
  505.8 1.9 collective-permute-start.20
  507.7 2.6 collective-permute-start.21
  510.3 5.7 %collective-permute-done.21 = f32[3,1,1024]{2,1,0:T(1,128)S(1)} collective-permute-done((f32[3,1,1024]{2,1,0:T(1,128)S(1)}, f32[3,1,1024]{2,1,0:T(1,128)S(1)}, u32[]{:S(2)}, u32[]{:S(2)}) %collective-permute-start.21) | collective-permute-done | bytes 12320 | tf_op jit(solution)/shard_map/ppermute | solution.py:24
  516.9 13.6 %concatenate.184 = f32[32769,16]{1,0:T(8,128)} pad(f32[32768,16]{1,0:T(8,128)} %all-gather.4.cloned.1.call-done, f32[]{:T(128)} %constant.38.clone.1), padding=1_0x0_0 | pad | bytes 4194372 | tf_op jit(solution)/shard_map/concatenate | solution.py:127
  530.6 12.9 %scatter_custom_fusion.1 = f32[16,4096]{0,1:T(8,128)S(1)} fusion(s32[512]{0:T(512)S(1)} %get-tuple-element.196, f32[]{:T(128)} %constant.38.clone.1, f32[]{:T(128)} %constant.109.clone.1, pred[512]{0:T(512)(128)(4,1)S(1)} %get-tuple-element.197, f32[32769,16]{1,0:T(8,128)} %concatenate.184, s32[1024]{0:T(1024)S(1)} %pad_clamp_fusion), kind=kCustom, calls=%fused_computation.9 | custom fusion | flops 16384 | bytes 2363976 | tf_op jit(solution)/shard_map/scatter-add | solution.py:134
  544.6 2.2 fusion.16
  (161 shorter events, 79.2 us)
Async XLA Ops:
  7.2 509.8 %all-gather.4.cloned.1.call-start = ((), (), s32[]{:S(2)}) async-start(), calls=%async_computation | async-start | bytes 16908288 | tf_op jit(solution)/shard_map/all_gather | solution.py:114
  8.1 398.2 %collective-permute-start.5 = (f32[3,1,1024]{2,1,0:T(1,128)S(1)}, f32[3,1,1024]{2,1,0:T(1,128)S(1)}, u32[]{:S(2)}, u32[]{:S(2)}) collective-permute-start(f32[3,1,1024]{2,1,0:T(1,128)S(1)} %get-tuple-element.249), channel_id=1, source_target_pairs={{0,4},{4,8},{8,12},{12,16},{16,20},{20,24},{24,28},{28,32},{32,36}... | collective-permute-start | bytes 36872 | tf_op jit(solution)/shard_map/ppermute | solution.py:22
  13.1 393.2 %collective-permute-start.7 = (f32[3,1,1024]{2,1,0:T(1,128)S(1)}, f32[3,1,1024]{2,1,0:T(1,128)S(1)}, u32[]{:S(2)}, u32[]{:S(2)}) collective-permute-start(f32[3,1,1024]{2,1,0:T(1,128)S(1)} %get-tuple-element.250), channel_id=1, source_target_pairs={{4,0},{8,4},{12,8},{16,12},{20,16},{24,20},{28,24},{32,28},{36,32}... | collective-permute-start | bytes 36872 | tf_op jit(solution)/shard_map/ppermute | solution.py:24
  16.5 83.6 %copy-start = (f32[16,4,1024]{2,1,0:T(4,128)S(1)}, f32[16,4,1024]{2,1,0:T(4,128)}, u32[]{:S(2)}) copy-start(f32[16,4,1024]{2,1,0:T(4,128)} %param.12) | copy-start | bytes 786436
  100.1 9.3 %copy-start.1 = (f32[3,4,1024]{2,1,0:T(4,128)S(1)}, f32[3,4,1024]{2,1,0:T(4,128)}, u32[]{:S(2)}) copy-start(f32[3,4,1024]{2,1,0:T(4,128)} %param.20) | copy-start | bytes 147460
  100.3 10.4 %copy-start.9 = (s32[256,1]{0,1:T(1,128)S(1)}, s32[256,1]{0,1:T(1,128)}, u32[]{:S(2)}) copy-start(s32[256,1]{0,1:T(1,128)} %param.18) | copy-start | bytes 3076
  100.5 301.3 %collective-permute-start = (f32[2,16,1,1024]{3,2,1,0:T(1,128)S(1)}, f32[2,16,1,1024]{3,2,1,0:T(1,128)S(1)}, u32[]{:S(2)}, u32[]{:S(2)}) collective-permute-start(f32[2,16,1,1024]{3,2,1,0:T(1,128)S(1)} %get-tuple-element.210), channel_id=1, source_target_pairs={{0,4},{4,8},{8,12},{12,16},{16,20},{20,24},{24,28},{28,32},{32,36}... | collective-permute-start | bytes 393224 | tf_op jit(solution)/shard_map/ppermute | solution.py:22
  107.5 294.3 %collective-permute-start.1 = (f32[2,16,1,1024]{3,2,1,0:T(1,128)S(1)}, f32[2,16,1,1024]{3,2,1,0:T(1,128)S(1)}, u32[]{:S(2)}, u32[]{:S(2)}) collective-permute-start(f32[2,16,1,1024]{3,2,1,0:T(1,128)S(1)} %get-tuple-element.211), channel_id=1, source_target_pairs={{4,0},{8,4},{12,8},{16,12},{20,16},{24,20},{28,24},{32,28},{36,32}... | collective-permute-start | bytes 393224 | tf_op jit(solution)/shard_map/ppermute | solution.py:24
  110.6 205.5 %copy-start.10 = (s32[256]{0:T(256)S(1)}, s32[256]{0:T(256)}, u32[]{:S(2)}) copy-start(s32[256]{0:T(256)} %param.19) | copy-start | bytes 3076
  401.9 4.6 collective-permute-start.2
  405.0 5.0 collective-permute-start.3
  410.7 25.0 %copy-start.3 = (f32[17,4,1024]{2,1,0:T(4,128)}, f32[17,4,1024]{2,1,0:T(4,128)S(1)}, u32[]{:S(2)}) copy-start(f32[17,4,1024]{2,1,0:T(4,128)S(1)} %fusion.6) | copy-start | bytes 835588
  410.7 12.9 %copy-start.5 = (f32[3,4,1024]{2,1,0:T(4,128)S(1)}, f32[3,4,1024]{2,1,0:T(4,128)}, u32[]{:S(2)}) copy-start(f32[3,4,1024]{2,1,0:T(4,128)} %param.21) | copy-start | bytes 147460
  410.8 25.9 %copy-start.2 = (f32[3,4,1024]{2,1,0:T(4,128)S(1)}, f32[3,4,1024]{2,1,0:T(4,128)}, u32[]{:S(2)}) copy-start(f32[3,4,1024]{2,1,0:T(4,128)} %constant.112.clone.1) | copy-start | bytes 147460
  423.6 12.9 %collective-permute-start.6 = (f32[8,1,1024]{2,1,0:T(1,128)S(1)}, f32[8,1,1024]{2,1,0:T(1,128)S(1)}, u32[]{:S(2)}, u32[]{:S(2)}) collective-permute-start(f32[8,1,1024]{2,1,0:T(1,128)S(1)} %get-tuple-element.213), channel_id=1, source_target_pairs={{4,0},{8,4},{12,8},{16,12},{20,16},{24,20},{28,24},{32,28},{36,32}... | collective-permute-start | bytes 98312 | tf_op jit(solution)/shard_map/ppermute | solution.py:24
  430.7 5.8 %collective-permute-start.4 = (f32[8,1,1024]{2,1,0:T(1,128)S(1)}, f32[8,1,1024]{2,1,0:T(1,128)S(1)}, u32[]{:S(2)}, u32[]{:S(2)}) collective-permute-start(f32[8,1,1024]{2,1,0:T(1,128)S(1)} %get-tuple-element.214), channel_id=1, source_target_pairs={{0,4},{4,8},{8,12},{12,16},{16,20},{20,24},{24,28},{28,32},{32,36}... | collective-permute-start | bytes 98312 | tf_op jit(solution)/shard_map/ppermute | solution.py:22
  437.0 8.9 %collective-permute-start.8 = (f32[3,1,1024]{2,1,0:T(1,128)S(1)}, f32[3,1,1024]{2,1,0:T(1,128)S(1)}, u32[]{:S(2)}, u32[]{:S(2)}) collective-permute-start(f32[3,1,1024]{2,1,0:T(1,128)S(1)} %get-tuple-element.245), channel_id=1, source_target_pairs={{0,4},{4,8},{8,12},{12,16},{16,20},{20,24},{24,28},{28,32},{32,36}... | collective-permute-start | bytes 36872 | tf_op jit(solution)/shard_map/ppermute | solution.py:22
  444.0 8.3 %collective-permute-start.9 = (f32[3,1,1024]{2,1,0:T(1,128)S(1)}, f32[3,1,1024]{2,1,0:T(1,128)S(1)}, u32[]{:S(2)}, u32[]{:S(2)}) collective-permute-start(f32[3,1,1024]{2,1,0:T(1,128)S(1)} %get-tuple-element.246), channel_id=1, source_target_pairs={{4,0},{8,4},{12,8},{16,12},{20,16},{24,20},{28,24},{32,28},{36,32}... | collective-permute-start | bytes 36872 | tf_op jit(solution)/shard_map/ppermute | solution.py:24
  452.7 4.4 collective-permute-start.10
  454.6 8.3 %collective-permute-start.11 = (f32[3,1,1024]{2,1,0:T(1,128)S(1)}, f32[3,1,1024]{2,1,0:T(1,128)S(1)}, u32[]{:S(2)}, u32[]{:S(2)}) collective-permute-start(f32[3,1,1024]{2,1,0:T(1,128)S(1)} %get-tuple-element.242), channel_id=1, source_target_pairs={{4,0},{8,4},{12,8},{16,12},{20,16},{24,20},{28,24},{32,28},{36,32}... | collective-permute-start | bytes 36872 | tf_op jit(solution)/shard_map/ppermute | solution.py:24
  463.3 4.4 collective-permute-start.12
  465.3 8.3 %collective-permute-start.13 = (f32[3,1,1024]{2,1,0:T(1,128)S(1)}, f32[3,1,1024]{2,1,0:T(1,128)S(1)}, u32[]{:S(2)}, u32[]{:S(2)}) collective-permute-start(f32[3,1,1024]{2,1,0:T(1,128)S(1)} %get-tuple-element.238), channel_id=1, source_target_pairs={{4,0},{8,4},{12,8},{16,12},{20,16},{24,20},{28,24},{32,28},{36,32}... | collective-permute-start | bytes 36872 | tf_op jit(solution)/shard_map/ppermute | solution.py:24
  473.9 4.4 collective-permute-start.14
  475.9 8.3 %collective-permute-start.15 = (f32[3,1,1024]{2,1,0:T(1,128)S(1)}, f32[3,1,1024]{2,1,0:T(1,128)S(1)}, u32[]{:S(2)}, u32[]{:S(2)}) collective-permute-start(f32[3,1,1024]{2,1,0:T(1,128)S(1)} %get-tuple-element.234), channel_id=1, source_target_pairs={{4,0},{8,4},{12,8},{16,12},{20,16},{24,20},{28,24},{32,28},{36,32}... | collective-permute-start | bytes 36872 | tf_op jit(solution)/shard_map/ppermute | solution.py:24
  484.5 4.4 collective-permute-start.16
  486.5 8.3 %collective-permute-start.17 = (f32[3,1,1024]{2,1,0:T(1,128)S(1)}, f32[3,1,1024]{2,1,0:T(1,128)S(1)}, u32[]{:S(2)}, u32[]{:S(2)}) collective-permute-start(f32[3,1,1024]{2,1,0:T(1,128)S(1)} %get-tuple-element.230), channel_id=1, source_target_pairs={{4,0},{8,4},{12,8},{16,12},{20,16},{24,20},{28,24},{32,28},{36,32}... | collective-permute-start | bytes 36872 | tf_op jit(solution)/shard_map/ppermute | solution.py:24
  495.1 4.4 collective-permute-start.18
  497.1 8.3 %collective-permute-start.19 = (f32[3,1,1024]{2,1,0:T(1,128)S(1)}, f32[3,1,1024]{2,1,0:T(1,128)S(1)}, u32[]{:S(2)}, u32[]{:S(2)}) collective-permute-start(f32[3,1,1024]{2,1,0:T(1,128)S(1)} %get-tuple-element.226), channel_id=1, source_target_pairs={{4,0},{8,4},{12,8},{16,12},{20,16},{24,20},{28,24},{32,28},{36,32}... | collective-permute-start | bytes 36872 | tf_op jit(solution)/shard_map/ppermute | solution.py:24
  505.8 4.5 collective-permute-start.20
  507.7 8.3 %collective-permute-start.21 = (f32[3,1,1024]{2,1,0:T(1,128)S(1)}, f32[3,1,1024]{2,1,0:T(1,128)S(1)}, u32[]{:S(2)}, u32[]{:S(2)}) collective-permute-start(f32[3,1,1024]{2,1,0:T(1,128)S(1)} %get-tuple-element.218), channel_id=1, source_target_pairs={{4,0},{8,4},{12,8},{16,12},{20,16},{24,20},{28,24},{32,28},{36,32}... | collective-permute-start | bytes 36872 | tf_op jit(solution)/shard_map/ppermute | solution.py:24
  543.5 0.9 slice-start
  543.5 1.1 copy-start.4
  543.5 1.1 copy-start.6
  543.5 1.1 copy-start.7
  543.5 1.0 copy-start.8
Sparse Core Ops, SparseCore 0:
  16.6 159.3 all-gather.3
where the time goes:
time: 559 us; the launch traced here: 554 us
  local copies, waits for them, and re-layouts  186 us (33%)
  blocking collectives  179 us (32%)
  starting transfers between devices  66.6 us (12%)
  other arithmetic  61.9 us (11%)
  waiting for transfers between devices  45.2 us (8%)
  between operations  14.9 us (3%)
    scatter x1, local copies, waits for them, and re-layouts, body(): jnp.zeros((slot_total + 1,), jnp.int32).at[slot_index].set(row_numbers)  120 us
    all_gather x1, blocking collectives, body(): lax.all_gather(tile_ids, 'wide', axis=0, tiled=True)  84.4 us
    all_gather x1, blocking collectives, body(): lax.all_gather(root_column, 'wide', axis=0, tiled=True)  82.4 us
    ppermute x11, waiting for transfers between devices, padded_2(): lax.ppermute(head, axis, [((i + 1) % count, i) for i in range(ends)])  45.2 us
    dynamic_slice x36, local copies, waits for them, and re-layouts, pick(): table[class_index]  44.3 us
    select_n x24, other arithmetic, pick(): jnp.where(matched, table[class_index], current)  39.1 us
    ppermute x11, starting transfers between devices, padded_2(): lax.ppermute(tail, axis, [(i, (i + 1) % count) for i in range(ends)])  37.9 us
    ppermute x11, starting transfers between devices, padded_2(): lax.ppermute(head, axis, [((i + 1) % count, i) for i in range(ends)])  28.6 us
  transfers between devices with their start and end apart: 23, of which 8 were waited for; matrix products, arithmetic and copies ran while one was open for 39% of the time, Pallas kernels for 0%

commit v1 on v0

v1 whole, which is shorter than its diff:
```python
import functools

import jax
import jax.numpy as jnp
from jax import lax
from jax.experimental import pallas as pl
from jax.experimental.pallas import tpu as pltpu
from jax.sharding import PartitionSpec as P

SWEEPS = 8
TIME_STEP = 0.25
STORAGE = 0.05
LEAKANCE = 0.5
PEERS = 8
CAP = 4
F32, BF16, I32 = jnp.float32, jnp.bfloat16, jnp.int32
MESH = pl.DeviceIdType.MESH
NT = (((1,), (1,)), ((), ()))


def roll(x, shift, axis):
    return pltpu.roll(x, shift % x.shape[axis], axis)


def iota(shape, axis):
    return lax.broadcasted_iota(I32, shape, axis)


def send(src, dst, send_sem, recv_sem, wide, narrow):
    copy = pltpu.make_async_remote_copy(
        src_ref=src,
        dst_ref=dst,
        send_sem=send_sem,
        recv_sem=recv_sem,
        device_id=(wide, narrow),
        device_id_type=MESH,
    )
    copy.start()
    return copy


def root_slots(uptake, tile, column, order):
    place = order(tile)
    cell_row = ((column // 128) % 8) * 4 + column // 1024
    cell_lane = column % 128
    count = tile.shape[1]
    aimed = iota((128, count), 0) == place
    earlier = iota((count, count), 0) < iota((count, count), 1)
    rank = jnp.dot(
        aimed.astype(F32).astype(BF16),
        earlier.astype(F32).astype(BF16),
        preferred_element_type=F32,
    )
    picks = jnp.concatenate(
        [(aimed & (rank == float(k))).astype(F32).astype(BF16) for k in range(CAP)], axis=0
    )
    high = uptake.astype(BF16)
    low = (uptake - high.astype(F32)).astype(BF16)
    line = iota((16, count), 0)
    extra = jnp.where(
        line == 0,
        cell_row.astype(F32),
        jnp.where(line == 1, cell_lane.astype(F32), 0.0),
    ).astype(BF16)
    base = jnp.concatenate([high, extra, low, jnp.zeros_like(extra)], axis=0)
    spread = lax.dot_general(base, picks, NT, preferred_element_type=F32)
    rows = spread[:32] + spread[32:]
    slots = jnp.concatenate([rows[:, 128 * k : 128 * (k + 1)] for k in range(CAP)], axis=0)
    return slots.T


def ring_left(tiles, lane):
    moved = [roll(v, 1, 1) for v in tiles]
    return [jnp.where(lane == 0, moved[t - 1], moved[t]) for t in range(len(tiles))]


def ring_right(tiles, lane):
    moved = [roll(v, -1, 1) for v in tiles]
    return [
        jnp.where(lane == 127, moved[(t + 1) % len(tiles)], moved[t]) for t in range(len(tiles))
    ]


def kernel(
    wide_count,
    narrow_count,
    head_ref,
    texture_ref,
    saturated_ref,
    shape_ref,
    capacity_ref,
    uptake_ref,
    tile_ref,
    column_ref,
    aquifer_ref,
    trans_ref,
    out_ref,
    aquifer_out_ref,
    table,
    soil,
    rest,
    part,
    face_out,
    face_in,
    slots,
    stage_1,
    turned,
    stage_2,
    patch,
    patches,
    drain,
    drains,
    coef,
    spread,
    slot_lines,
    slots_sent,
    slots_got,
    turned_sent,
    turned_got,
    patch_sent,
    patch_got,
    drain_sent,
    drain_got,
    face_sent,
    face_got,
    slab_sent,
    slab_got,
):
    w = lax.axis_index("wide")
    n = lax.axis_index("narrow")
    depth = wide_count // PEERS
    my_z, my_peer = w // PEERS, w % PEERS
    bottom = n == narrow_count - 1
    around = (-2, -1, 1, 2)

    def wide_at(step):
        return (w + step + wide_count) % wide_count

    barrier = pltpu.get_barrier_semaphore()

    def greet(wide, narrow):
        pl.semaphore_signal(barrier, inc=1, device_id=(wide, narrow), device_id_type=MESH)

    for j in range(1, PEERS):
        greet(my_z * PEERS + (my_peer + j) % PEERS, n)
    for j in range(1, depth):
        greet(((my_z + j) % depth) * PEERS + my_peer, n)
    for step in around:
        greet(wide_at(step), n)
    greet(w, (n + 1) % narrow_count)
    greet(w, (n + narrow_count - 1) % narrow_count)

    @pl.when(jnp.logical_not(bottom))
    def _():
        for step in (-2, -1, 0, 1, 2):
            greet(wide_at(step), narrow_count - 1)

    made = root_slots(
        uptake_ref[...],
        tile_ref[...],
        column_ref[...],
        lambda tile: (tile % PEERS) * depth + tile // PEERS,
    )
    slots[...] = made.reshape(PEERS, depth, 128)

    lane4 = iota((4, 128), 1)
    for a in range(6):
        source = aquifer_ref if a < 3 else trans_ref
        first = (a % 3) * 32
        here = source[pl.ds(pl.multiple_of(first + 8 * n, 8), 8), :]
        after = source[pl.ds(pl.multiple_of(first + 8 * jnp.minimum(n + 1, 3), 8), 8), :]
        before = source[pl.ds(pl.multiple_of(first + 8 * jnp.maximum(n - 1, 0), 8), 8), :]
        after = jnp.where(n < narrow_count - 1, after[0:4], 0.0)
        before = jnp.where(n > 0, before[4:8], 0.0)
        patch[3 * a] = here[0:4]
        patch[3 * a + 1] = here[4:8]
        patch[3 * a + 2] = jnp.where(lane4 < 64, after, before)
    for a in range(18):
        patches[a, 2] = patch[a]
        patches[a, 5] = jnp.zeros((4, 128), F32)
    for t in range(3):
        drains[t, 5] = jnp.zeros((4, 128), F32)

    @pl.when(bottom)
    def _():
        pl.semaphore_wait(barrier, PEERS - 1 + depth - 1 + 6 + 5 * (narrow_count - 1))

    @pl.when(jnp.logical_not(bottom))
    def _():
        pl.semaphore_wait(barrier, PEERS - 1 + depth - 1 + 6)

    first_stage = []
    for j in range(1, PEERS):
        peer = (my_peer + j) % PEERS
        first_stage.append(
            send(
                slots.at[peer],
                stage_1.at[my_peer],
                slots_sent.at[j],
                slots_got.at[j],
                my_z * PEERS + peer,
                n,
            )
        )
    stage_1[my_peer] = slots[my_peer]

    patch_copies = []
    for i, step in enumerate(around):
        patch_copies.append(
            send(
                patch,
                patches.at[:, 2 - step],
                patch_sent.at[i],
                patch_got.at[i],
                wide_at(step),
                n,
            )
        )

    table[...] = jnp.zeros_like(table)
    table[0:1, 0:12] = saturated_ref[...]
    table[8:9, 0:12] = shape_ref[...]
    table[16:17, 0:12] = capacity_ref[...]

    def look_up(row, index):
        values = jnp.broadcast_to(table[row : row + 1, :], index.shape)
        return jnp.take_along_axis(values, index, axis=1, mode="promise_in_bounds")

    def conduct_layer(z, carry):
        here = pl.ds(pl.multiple_of(z * 32, 32), 32)
        there = pl.ds(pl.multiple_of(z * 32 + 32, 32), 32)
        head = head_ref[here, :]
        index = texture_ref[here, :]
        soil[0, there, :] = head
        soil[1, there, :] = look_up(0, index) * jnp.exp(look_up(8, index) * jnp.minimum(head, 0.0))
        rest[here, :] = TIME_STEP / look_up(16, index)
        return carry

    lax.fori_loop(0, 16, conduct_layer, 0)

    @pl.when(bottom)
    def _():
        flow = soil[1, 512:544, :] * (soil[0, 512:544, :] - aquifer_ref[0:32, :] + 1.0)
        for q in range(4):
            drain[q, 0] = flow[8 * q : 8 * q + 4]
            drain[q, 1] = flow[8 * q + 4 : 8 * q + 8]
            after = flow[8 * q + 8 : 8 * q + 12] if q < 3 else jnp.zeros((4, 128), F32)
            before = flow[8 * q - 4 : 8 * q] if q > 0 else jnp.zeros((4, 128), F32)
            drain[q, 2] = jnp.where(lane4 < 64, after, before)
        for step in (0, 1, -1, 2, -2):
            for q in range(4):
                if step == 0 and q == 3:
                    continue
                send(
                    drain.at[q],
                    drains.at[:, 2 - step],
                    drain_sent.at[step + 2, q],
                    drain_got.at[2 - step],
                    wide_at(step),
                    q,
                )
        drains[:, 2] = drain[3]

    for i, first in ((0, 35), (1, 32)):
        for v in range(2):
            face_out[i, v] = soil[v, pl.ds(first, 128, stride=4), :]
    face_copies = [
        send(
            face_out.at[i],
            face_in.at[i],
            face_sent.at[i],
            face_got.at[i],
            wide_at(1 if i == 0 else -1),
            n,
        )
        for i in range(2)
    ]
    slab_copies = [
        send(
            soil.at[:, pl.ds(512, 32)],
            soil.at[:, pl.ds(0, 32)],
            slab_sent.at[0],
            slab_got.at[0],
            w,
            (n + 1) % narrow_count,
        ),
        send(
            soil.at[:, pl.ds(32, 32)],
            soil.at[:, pl.ds(544, 32)],
            slab_sent.at[1],
            slab_got.at[1],
            w,
            (n + narrow_count - 1) % narrow_count,
        ),
    ]

    for j in range(1, PEERS):
        other = (my_peer + PEERS - j) % PEERS
        pltpu.make_async_remote_copy(
            src_ref=slots.at[other],
            dst_ref=stage_1.at[other],
            send_sem=slots_sent.at[j],
            recv_sem=slots_got.at[j],
            device_id=(w, n),
            device_id_type=MESH,
        ).wait_recv()
    for z in range(depth):
        for p in range(PEERS):
            turned[z, p : p + 1] = stage_1[p, z : z + 1]
    second_stage = []
    for j in range(1, depth):
        other = (my_z + j) % depth
        second_stage.append(
            send(
                turned.at[other],
                stage_2.at[my_z],
                turned_sent.at[j],
                turned_got.at[j],
                other * PEERS + my_peer,
                n,
            )
        )
    stage_2[my_z] = turned[my_z]

    for copy in slab_copies + face_copies:
        copy.wait_recv()

    @pl.when(n == 0)
    def _():
        soil[0, 0:32, :] = soil[0, 32:64, :]
        soil[1, 0:32, :] = -soil[1, 32:64, :]

    @pl.when(bottom)
    def _():
        soil[0, 544:576, :] = aquifer_ref[0:32, :]
        soil[1, 544:576, :] = soil[1, 512:544, :]

    row = iota((32, 128), 0)
    lane = iota((32, 128), 1)
    x = row % 4
    sub8 = iota((8, 128), 0)
    left_open = jnp.where((x == 0) & (w == 0), 0.0, 0.5)
    right_open = jnp.where(w == wide_count - 1, 0.0, 0.5)
    along_open = jnp.where((lane == 0) & (row < 4), 0.0, 0.5)

    def widened(side, v, z):
        pieces = []
        for j in range(4):
            one = face_in[side, v, pl.ds(z * 8 + 2 * j, 1), :]
            two = face_in[side, v, pl.ds(z * 8 + 2 * j + 1, 1), :]
            pieces.append(
                jnp.where(
                    sub8 < 4, jnp.broadcast_to(one, (8, 128)), jnp.broadcast_to(two, (8, 128))
                )
            )
        return jnp.concatenate(pieces, axis=0)

    def previous_column(v):
        moved = roll(v, 1, 1)
        return jnp.where(lane == 0, roll(moved, 4, 0), moved)

    def balance_layer(z, carry):
        over = pl.ds(pl.multiple_of(z * 32, 32), 32)
        here = pl.ds(pl.multiple_of(z * 32 + 32, 32), 32)
        under = pl.ds(pl.multiple_of(z * 32 + 64, 32), 32)
        head, cond = soil[0, here, :], soil[1, here, :]
        vertical_in = 0.5 * (soil[1, over, :] + cond) * (soil[0, over, :] - head + 1.0)
        vertical_out = 0.5 * (cond + soil[1, under, :]) * (head - soil[0, under, :] + 1.0)
        head_left = jnp.where(x == 0, widened(0, 0, z), roll(head, 1, 0))
        cond_left = jnp.where(x == 0, widened(0, 1, z), roll(cond, 1, 0))
        across_in = left_open * (cond_left + cond) * (head_left - head)
        last = right_open * (cond + widened(1, 1, z)) * (head - widened(1, 0, z))
        across_out = jnp.where(x == 3, last, roll(across_in, -1, 0))
        along_in = along_open * (previous_column(cond) + cond) * (previous_column(head) - head)
        moved = roll(along_in, -1, 1)
        along_out = jnp.where(lane == 127, roll(moved, -4, 0), moved)
        balance = (
            (vertical_in - vertical_out) + (across_in - across_out) + (along_in - along_out)
        )
        at = pl.ds(pl.multiple_of(z * 32, 32), 32)
        part[at, :] = head + balance * rest[at, :]
        return carry

    lax.fori_loop(0, 16, balance_layer, 0)

    for i, step in enumerate(around):
        pltpu.make_async_remote_copy(
            src_ref=patch,
            dst_ref=patches.at[:, 2 - step],
            send_sem=patch_sent.at[i],
            recv_sem=patch_got.at[i],
            device_id=(w, n),
            device_id_type=MESH,
        ).wait_recv()
    for step in (-2, -1, 0, 1, 2):

        def wait_drain(step=step):
            pltpu.make_async_remote_copy(
                src_ref=drain.at[0],
                dst_ref=drains.at[:, 2 - step],
                send_sem=drain_sent.at[step + 2, 0],
                recv_sem=drain_got.at[2 - step],
                device_id=(w, n),
                device_id_type=MESH,
            ).wait_recv()

        if step == 0:
            pl.when(jnp.logical_not(bottom))(wait_drain)
        else:
            wait_drain()

    lane24 = iota((24, 128), 1)
    line = iota((24, 128), 0) + 4 * w - 8
    inside = jnp.where((line >= 0) & (line < 4 * wide_count), 1.0, 0.0)
    after_open = jnp.where(n < narrow_count - 1, 1.0, 0.0)
    before_open = jnp.where(n > 0, 1.0, 0.0)
    inside_halo = inside * jnp.where(lane24 < 64, after_open, before_open)

    def stacked(ref, a):
        return jnp.concatenate([ref[a, s] for s in range(6)], axis=0)

    heads = [[stacked(patches, 3 * l + t) * inside for t in range(3)] for l in range(3)]
    flows = [stacked(drains, t) for t in range(3)]
    for l in range(3):
        trans = [stacked(patches, 9 + 3 * l + t) * inside for t in range(3)]
        wests, easts = ring_left(trans, lane24), ring_right(trans, lane24)
        for t in range(3):
            centre = trans[t]
            north = 0.5 * (centre + roll(centre, 1, 0))
            south = 0.5 * (centre + roll(centre, -1, 0))
            west = 0.5 * (centre + wests[t])
            east = 0.5 * (centre + easts[t])
            links = 2.0 if l == 1 else 1.0
            divisor = STORAGE + north + south + west + east + LEAKANCE * links
            inverse = (inside_halo if t == 2 else inside) / divisor
            source = STORAGE * heads[l][t]
            if l == 0:
                source = source + flows[t]
            k = 3 * l + t
            coef[0, k] = north * inverse
            coef[1, k] = south * inverse
            coef[2, k] = west * inverse
            coef[3, k] = east * inverse
            coef[4, k] = LEAKANCE * inverse
            coef[5, k] = source * inverse

    def sweep(_, flat):
        now = [flat[3 * l : 3 * l + 3] for l in range(3)]
        later = []
        for l in range(3):
            wests, easts = ring_left(now[l], lane24), ring_right(now[l], lane24)
            for t in range(3):
                k = 3 * l + t
                centre = now[l][t]
                if l == 1:
                    vertical = now[0][t] + now[2][t]
                else:
                    vertical = now[1][t]
                later.append(
                    coef[5, k]
                    + coef[0, k] * roll(centre, 1, 0)
                    + coef[1, k] * roll(centre, -1, 0)
                    + coef[2, k] * wests[t]
                    + coef[3, k] * easts[t]
                    + coef[4, k] * vertical
                )
        return tuple(later)

    flat = lax.fori_loop(0, SWEEPS, sweep, tuple(v for layer in heads for v in layer))
    for l in range(3):
        aquifer_out_ref[8 * l : 8 * l + 8, :] = jnp.concatenate(
            [flat[3 * l][8:12], flat[3 * l + 1][8:12]], axis=0
        )

    for j in range(1, depth):
        other = (my_z + depth - j) % depth
        pltpu.make_async_remote_copy(
            src_ref=turned.at[other],
            dst_ref=stage_2.at[other],
            send_sem=turned_sent.at[j],
            recv_sem=turned_got.at[j],
            device_id=(w, n),
            device_id_type=MESH,
        ).wait_recv()
    slot_lines[...] = stage_2[...].reshape(128, 128).T
    lanes = iota((128, 128), 0).astype(F32)
    rows = iota((32, 128), 0).astype(F32)
    target = jnp.concatenate(
        [
            (lanes == slot_lines[32 * k + 17 : 32 * k + 18, :]).astype(F32).astype(BF16)
            for k in range(CAP)
        ],
        axis=1,
    )
    for k in range(CAP):
        hit = rows == slot_lines[32 * k + 16 : 32 * k + 17, :]

        def place(z, carry, k=k, hit=hit):
            value = slot_lines[pl.ds(32 * k + z, 1), :]
            value = jnp.where(hit, jnp.broadcast_to(value, (32, 128)), 0.0)
            high = value.astype(BF16)
            low = (value - high.astype(F32)).astype(BF16)
            spread[pl.ds(pl.multiple_of(z * 32, 32), 32), 128 * k : 128 * k + 128] = high
            spread[pl.ds(pl.multiple_of(z * 32 + 512, 32), 32), 128 * k : 128 * k + 128] = low
            return carry

        lax.fori_loop(0, 16, place, 0)
    taken = lax.dot_general(spread[...], target, NT, preferred_element_type=F32)
    out_ref[...] = part[...] - (taken[:512] + taken[512:]) * rest[...]

    for copy in first_stage + patch_copies + face_copies + slab_copies + second_stage:
        copy.wait_send()

    @pl.when(bottom)
    def _():
        for step in (0, 1, -1, 2, -2):
            for q in range(4):
                if step == 0 and q == 3:
                    continue
                pltpu.make_async_remote_copy(
                    src_ref=drain.at[q],
                    dst_ref=drains.at[:, 2 - step],
                    send_sem=drain_sent.at[step + 2, q],
                    recv_sem=drain_got.at[2 - step],
                    device_id=(w, n),
                    device_id_type=MESH,
                ).wait_send()


def rows_of(a):
    k = a.shape[0]
    return a.reshape(k, 4, 8, 128).transpose(0, 2, 1, 3).reshape(k * 32, 128)


def grid_of(a, k, columns):
    return a.reshape(k, columns // 128, 4, 128).transpose(0, 2, 1, 3).reshape(k, 4, columns)


def body(
    pressure_head,
    texture,
    saturated_table,
    shape_table,
    capacity_table,
    uptake,
    root_tile,
    root_column,
    aquifer_head,
    transmissivity,
):
    wide_count = lax.axis_size("wide")
    narrow_count = lax.axis_size("narrow")
    depth = wide_count // PEERS
    dma = pltpu.SemaphoreType.DMA
    out, aquifer_out = pl.pallas_call(
        functools.partial(kernel, wide_count, narrow_count),
        out_shape=(
            jax.ShapeDtypeStruct((512, 128), F32),
            jax.ShapeDtypeStruct((24, 128), F32),
        ),
        in_specs=[pl.BlockSpec(memory_space=pltpu.VMEM)] * 10,
        out_specs=[pl.BlockSpec(memory_space=pltpu.VMEM)] * 2,
        scratch_shapes=[
            pltpu.VMEM((24, 128), F32),
            pltpu.VMEM((2, 576, 128), F32),
            pltpu.VMEM((512, 128), F32),
            pltpu.VMEM((512, 128), F32),
            pltpu.VMEM((2, 2, 128, 128), F32),
            pltpu.VMEM((2, 2, 128, 128), F32),
            pltpu.VMEM((PEERS, depth, 128), F32),
            pltpu.VMEM((PEERS, depth, 128), F32),
            pltpu.VMEM((depth, PEERS, 128), F32),
            pltpu.VMEM((depth, PEERS, 128), F32),
            pltpu.VMEM((18, 4, 128), F32),
            pltpu.VMEM((18, 6, 4, 128), F32),
            pltpu.VMEM((4, 3, 4, 128), F32),
            pltpu.VMEM((3, 6, 4, 128), F32),
            pltpu.VMEM((6, 9, 24, 128), F32),
            pltpu.VMEM((1024, 512), BF16),
            pltpu.VMEM((128, 128), F32),
            dma((PEERS,)),
            dma((PEERS,)),
            dma((depth,)),
            dma((depth,)),
            dma((4,)),
            dma((4,)),
            dma((5, 4)),
            dma((5,)),
            dma((2,)),
            dma((2,)),
            dma((2,)),
            dma((2,)),
        ],
        compiler_params=pltpu.CompilerParams(
            collective_id=0, has_side_effects=True, vmem_limit_bytes=32 * 1024 * 1024
        ),
        name="coupled_step",
    )(
        rows_of(pressure_head),
        rows_of(texture),
        saturated_table.reshape(1, -1),
        shape_table.reshape(1, -1),
        capacity_table.reshape(1, -1),
        uptake.T,
        root_tile.reshape(1, -1),
        root_column.reshape(1, -1),
        rows_of(aquifer_head),
        rows_of(transmissivity),
    )
    return grid_of(out, 16, 1024), grid_of(aquifer_out, 3, 256)


def solution(mesh):
    in_specs = (
        P("narrow", "wide", None),
        P("narrow", "wide", None),
        P(),
        P(),
        P(),
        P("wide", "narrow"),
        P("wide", None),
        P("wide"),
        P(None, "wide", None),
        P(None, "wide", None),
    )
    out_specs = (P("narrow", "wide", None), P(None, "wide", "narrow"))
    return jax.shard_map(body, mesh=mesh, in_specs=in_specs, out_specs=out_specs, check_vma=False)
```

time: 559 us -> 36.2 us (0.06)
  the two profiles are of different devices: /device:TPU:121 before, /device:TPU:1 now
where the time goes in v1:
time: 36.2 us; the launch traced here: 35.8 us
  Pallas kernels  28.3 us (78%)
  local copies, waits for them, and re-layouts  6.8 us (19%)
  between operations  0.69 us (2%)
    pallas_call x1, Pallas kernels, body(): pl.pallas_call(functools.partial(kernel, wide_count, narrow_count), out_s...  28.3 us
    unnamed x22, local copies, waits for them, and re-layouts  6.8 us

profile of v1, /device:TPU:1, one launch (start us, length us, event | category | flops | bytes accessed | tf_op | source)
XLA Modules:
  0.0 35.8 jit_solution(567358461366098873)
XLA Ops:
  0.6 0.0 copy-start.4
  0.6 0.0 copy-start.6
  0.7 0.0 copy-start.5
  0.7 0.0 copy-start.7
  0.7 0.7 %copy-done.4 = f32[256,16]{0,1:T(8,128)S(1)} copy-done((f32[256,16]{0,1:T(8,128)S(1)}, f32[256,16]{0,1:T(8,128)}, u32[]{:S(2)}) %copy-start.4) | copy-done | bytes 16408
  1.4 0.0 copy-done.6
  1.4 0.0 copy-done.5
  1.4 0.0 copy-done.7
  1.4 0.0 copy-start
  1.4 0.9 %copy-done = f32[16,4,1024]{2,1,0:T(4,128)S(1)} copy-done((f32[16,4,1024]{2,1,0:T(4,128)S(1)}, f32[16,4,1024]{2,1,0:T(4,128)}, u32[]{:S(2)}) %copy-start) | copy-done | bytes 262168
  2.3 0.0 copy-start.1
  2.3 0.9 %copy-done.1 = s32[16,4,1024]{2,1,0:T(4,128)S(1)} copy-done((s32[16,4,1024]{2,1,0:T(4,128)S(1)}, s32[16,4,1024]{2,1,0:T(4,128)}, u32[]{:S(2)}) %copy-start.1) | copy-done | bytes 262168
  3.3 0.0 copy-start.2
  3.3 0.8 %copy-done.2 = f32[3,4,1024]{2,1,0:T(4,128)S(1)} copy-done((f32[3,4,1024]{2,1,0:T(4,128)S(1)}, f32[3,4,1024]{2,1,0:T(4,128)}, u32[]{:S(2)}) %copy-start.2) | copy-done | bytes 49176
  4.1 0.0 copy-start.3
  4.1 0.8 %copy-done.3 = f32[3,4,1024]{2,1,0:T(4,128)S(1)} copy-done((f32[3,4,1024]{2,1,0:T(4,128)S(1)}, f32[3,4,1024]{2,1,0:T(4,128)}, u32[]{:S(2)}) %copy-start.3) | copy-done | bytes 49176
  4.9 0.0 copy-start.8
  4.9 0.7 %copy-done.8 = f32[12]{0:T(128)S(1)} copy-done((f32[12]{0:T(128)S(1)}, f32[12]{0:T(128)}, u32[]{:S(2)}) %copy-start.8) | copy-done | bytes 72
  5.5 0.0 copy-start.9
  5.5 0.7 %copy-done.9 = f32[12]{0:T(128)S(1)} copy-done((f32[12]{0:T(128)S(1)}, f32[12]{0:T(128)}, u32[]{:S(2)}) %copy-start.9) | copy-done | bytes 72
  6.2 28.3 %coupled_step.1 = (f32[512,128]{1,0:T(8,128)S(1)}, f32[24,128]{1,0:T(8,128)S(1)}) custom-call(f32[512,128]{1,0:T(8,128)S(1)} %bitcast.36, s32[512,128]{1,0:T(8,128)S(1)} %bitcast.37, f32[1,12]{1,0:T(1,128)S(1)} %bitcast.45, f32[1,12]{1,0:T(1,128)S(1)} %bitcast.46, f32[1,12]{1,0:T(1,128)S(1)} %bitcast.47, f32[16,256]{1,0:T(8,128)S(1)} %bitcast.41, ...), custom_call_target="tpu_custom_call" | custom-call | tf_op jit(solution)/shard_map/coupled_step/pallas_call | solution.py:555
  34.5 0.7 %copy.20 = f32[16,4,1024]{2,1,0:T(4,128)} copy(f32[16,4,1024]{2,1,0:T(4,128)S(1)} %bitcast.38) | data formatting | bytes 524288
  35.2 0.6 %copy.21 = f32[3,4,256]{2,1,0:T(4,128)} copy(f32[3,4,256]{2,1,0:T(4,128)S(1)} %bitcast.42) | data formatting | bytes 24576
Async XLA Ops:
  0.6 0.7 %copy-start.4 = (f32[256,16]{0,1:T(8,128)S(1)}, f32[256,16]{0,1:T(8,128)}, u32[]{:S(2)}) copy-start(f32[256,16]{0,1:T(8,128)} %param.15) | copy-start | bytes 49156
  0.6 0.7 %copy-start.6 = (s32[256]{0:T(256)S(1)}, s32[256]{0:T(256)}, u32[]{:S(2)}) copy-start(s32[256]{0:T(256)} %param.17) | copy-start | bytes 3076
  0.7 0.7 %copy-start.5 = (s32[256,1]{0,1:T(1,128)S(1)}, s32[256,1]{0,1:T(1,128)}, u32[]{:S(2)}) copy-start(s32[256,1]{0,1:T(1,128)} %param.16) | copy-start | bytes 3076
  0.7 0.7 %copy-start.7 = (f32[12]{0:T(128)S(1)}, f32[12]{0:T(128)}, u32[]{:S(2)}) copy-start(f32[12]{0:T(128)} %param.12) | copy-start | bytes 148
  1.4 1.0 %copy-start = (f32[16,4,1024]{2,1,0:T(4,128)S(1)}, f32[16,4,1024]{2,1,0:T(4,128)}, u32[]{:S(2)}) copy-start(f32[16,4,1024]{2,1,0:T(4,128)} %param.10) | copy-start | bytes 786436
  2.3 0.9 %copy-start.1 = (s32[16,4,1024]{2,1,0:T(4,128)S(1)}, s32[16,4,1024]{2,1,0:T(4,128)}, u32[]{:S(2)}) copy-start(s32[16,4,1024]{2,1,0:T(4,128)} %param.11) | copy-start | bytes 786436
  3.3 0.8 %copy-start.2 = (f32[3,4,1024]{2,1,0:T(4,128)S(1)}, f32[3,4,1024]{2,1,0:T(4,128)}, u32[]{:S(2)}) copy-start(f32[3,4,1024]{2,1,0:T(4,128)} %param.18) | copy-start | bytes 147460
  4.1 0.8 %copy-start.3 = (f32[3,4,1024]{2,1,0:T(4,128)S(1)}, f32[3,4,1024]{2,1,0:T(4,128)}, u32[]{:S(2)}) copy-start(f32[3,4,1024]{2,1,0:T(4,128)} %param.19) | copy-start | bytes 147460
  4.9 0.7 %copy-start.8 = (f32[12]{0:T(128)S(1)}, f32[12]{0:T(128)}, u32[]{:S(2)}) copy-start(f32[12]{0:T(128)} %param.13) | copy-start | bytes 148
  5.5 0.7 %copy-start.9 = (f32[12]{0:T(128)S(1)}, f32[12]{0:T(128)}, u32[]{:S(2)}) copy-start(f32[12]{0:T(128)} %param.14) | copy-start | bytes 148

commit v2 on v1

--- a/solution.py
+++ b/solution.py
@@ -84,6 +84,18 @@
 def kernel(
     wide_count,
     narrow_count,
+    head_hbm,
+    texture_hbm,
+    saturated_hbm,
+    shape_hbm,
+    capacity_hbm,
+    uptake_hbm,
+    tile_hbm,
+    column_hbm,
+    aquifer_hbm,
+    trans_hbm,
+    out_ref,
+    aquifer_out_ref,
     head_ref,
     texture_ref,
     saturated_ref,
@@ -94,8 +106,6 @@
     column_ref,
     aquifer_ref,
     trans_ref,
-    out_ref,
-    aquifer_out_ref,
     table,
     soil,
     rest,
@@ -113,6 +123,7 @@
     coef,
     spread,
     slot_lines,
+    load_done,
     slots_sent,
     slots_got,
     turned_sent,
@@ -136,6 +147,15 @@
     def wide_at(step):
         return (w + step + wide_count) % wide_count
 
+    order = (6, 7, 5, 8, 9, 0, 1, 2, 3, 4)
+    held = (head_ref, texture_ref, saturated_ref, shape_ref, capacity_ref, uptake_ref, tile_ref)
+    held += (column_ref, aquifer_ref, trans_ref)
+    far = (head_hbm, texture_hbm, saturated_hbm, shape_hbm, capacity_hbm, uptake_hbm, tile_hbm)
+    far += (column_hbm, aquifer_hbm, trans_hbm)
+    loads = [pltpu.make_async_copy(far[i], held[i], load_done.at[i]) for i in range(10)]
+    for i in order:
+        loads[i].start()
+
     barrier = pltpu.get_barrier_semaphore()
 
     def greet(wide, narrow):
@@ -155,6 +175,9 @@
         for step in (-2, -1, 0, 1, 2):
             greet(wide_at(step), narrow_count - 1)
 
+    for i in (6, 7, 5):
+        loads[i].wait()
+
     made = root_slots(
         uptake_ref[...],
         tile_ref[...],
@@ -163,6 +186,8 @@
     )
     slots[...] = made.reshape(PEERS, depth, 128)
 
+    for i in (8, 9):
+        loads[i].wait()
     lane4 = iota((4, 128), 1)
     for a in range(6):
         source = aquifer_ref if a < 3 else trans_ref
@@ -217,6 +242,8 @@
             )
         )
 
+    for i in (0, 1, 2, 3, 4):
+        loads[i].wait()
     table[...] = jnp.zeros_like(table)
     table[0:1, 0:12] = saturated_ref[...]
     table[8:9, 0:12] = shape_ref[...]
@@ -558,9 +585,19 @@
             jax.ShapeDtypeStruct((512, 128), F32),
             jax.ShapeDtypeStruct((24, 128), F32),
         ),
-        in_specs=[pl.BlockSpec(memory_space=pltpu.VMEM)] * 10,
+        in_specs=[pl.BlockSpec(memory_space=pltpu.HBM)] * 10,
         out_specs=[pl.BlockSpec(memory_space=pltpu.VMEM)] * 2,
         scratch_shapes=[
+            pltpu.VMEM((512, 128), F32),
+            pltpu.VMEM((512, 128), I32),
+            pltpu.VMEM((1, 12), F32),
+            pltpu.VMEM((1, 12), F32),
+            pltpu.VMEM((1, 12), F32),
+            pltpu.VMEM((16, 256), F32),
+            pltpu.VMEM((1, 256), I32),
+            pltpu.VMEM((1, 256), I32),
+            pltpu.VMEM((96, 128), F32),
+            pltpu.VMEM((96, 128), F32),
             pltpu.VMEM((24, 128), F32),
             pltpu.VMEM((2, 576, 128), F32),
             pltpu.VMEM((512, 128), F32),
@@ -578,6 +615,7 @@
             pltpu.VMEM((6, 9, 24, 128), F32),
             pltpu.VMEM((1024, 512), BF16),
             pltpu.VMEM((128, 128), F32),
+            dma((10,)),
             dma((PEERS,)),
             dma((PEERS,)),
             dma((depth,)),

time: 36.2 us -> 36.5 us (level)
  no operation moved by 1% of the time
where the time goes in v2:
time: 36.5 us; the launch traced here: 36.1 us
  Pallas kernels  28.6 us (78%)
  local copies, waits for them, and re-layouts  6.8 us (19%)
  between operations  0.69 us (2%)
    pallas_call x1, Pallas kernels, body(): pl.pallas_call(functools.partial(kernel, wide_count, narrow_count), out_s...  28.6 us
    unnamed x22, local copies, waits for them, and re-layouts  6.8 us

profile of v2, /device:TPU:1, one launch (start us, length us, event | category | flops | bytes accessed | tf_op | source)
XLA Modules:
  0.0 36.1 jit_solution(5003069964365183509)
XLA Ops:
  0.6 0.0 copy-start.4
  0.6 0.0 copy-start.6
  0.7 0.0 copy-start.5
  0.7 0.0 copy-start.7
  0.7 0.7 %copy-done.4 = f32[256,16]{0,1:T(8,128)S(1)} copy-done((f32[256,16]{0,1:T(8,128)S(1)}, f32[256,16]{0,1:T(8,128)}, u32[]{:S(2)}) %copy-start.4) | copy-done | bytes 16408
  1.4 0.0 copy-done.6
  1.4 0.0 copy-done.5
  1.4 0.0 copy-done.7
  1.4 0.0 copy-start
  1.4 0.9 %copy-done = f32[16,4,1024]{2,1,0:T(4,128)S(1)} copy-done((f32[16,4,1024]{2,1,0:T(4,128)S(1)}, f32[16,4,1024]{2,1,0:T(4,128)}, u32[]{:S(2)}) %copy-start) | copy-done | bytes 262168
  2.3 0.0 copy-start.1
  2.3 0.9 %copy-done.1 = s32[16,4,1024]{2,1,0:T(4,128)S(1)} copy-done((s32[16,4,1024]{2,1,0:T(4,128)S(1)}, s32[16,4,1024]{2,1,0:T(4,128)}, u32[]{:S(2)}) %copy-start.1) | copy-done | bytes 262168
  3.3 0.0 copy-start.2
  3.3 0.8 %copy-done.2 = f32[3,4,1024]{2,1,0:T(4,128)S(1)} copy-done((f32[3,4,1024]{2,1,0:T(4,128)S(1)}, f32[3,4,1024]{2,1,0:T(4,128)}, u32[]{:S(2)}) %copy-start.2) | copy-done | bytes 49176
  4.1 0.0 copy-start.3
  4.1 0.8 %copy-done.3 = f32[3,4,1024]{2,1,0:T(4,128)S(1)} copy-done((f32[3,4,1024]{2,1,0:T(4,128)S(1)}, f32[3,4,1024]{2,1,0:T(4,128)}, u32[]{:S(2)}) %copy-start.3) | copy-done | bytes 49176
  4.9 0.0 copy-start.8
  4.9 0.7 %copy-done.8 = f32[12]{0:T(128)S(1)} copy-done((f32[12]{0:T(128)S(1)}, f32[12]{0:T(128)}, u32[]{:S(2)}) %copy-start.8) | copy-done | bytes 72
  5.5 0.0 copy-start.9
  5.5 0.7 %copy-done.9 = f32[12]{0:T(128)S(1)} copy-done((f32[12]{0:T(128)S(1)}, f32[12]{0:T(128)}, u32[]{:S(2)}) %copy-start.9) | copy-done | bytes 72
  6.2 28.6 %coupled_step.1 = (f32[512,128]{1,0:T(8,128)S(1)}, f32[24,128]{1,0:T(8,128)S(1)}) custom-call(f32[512,128]{1,0:T(8,128)S(1)} %bitcast.36, s32[512,128]{1,0:T(8,128)S(1)} %bitcast.37, f32[1,12]{1,0:T(1,128)S(1)} %bitcast.45, f32[1,12]{1,0:T(1,128)S(1)} %bitcast.46, f32[1,12]{1,0:T(1,128)S(1)} %bitcast.47, f32[16,256]{1,0:T(8,128)S(1)} %bitcast.41, ...), custom_call_target="tpu_custom_call" | custom-call | tf_op jit(solution)/shard_map/coupled_step/pallas_call | solution.py:582
  34.8 0.7 %copy.20 = f32[16,4,1024]{2,1,0:T(4,128)} copy(f32[16,4,1024]{2,1,0:T(4,128)S(1)} %bitcast.38) | data formatting | bytes 524288
  35.5 0.6 %copy.21 = f32[3,4,256]{2,1,0:T(4,128)} copy(f32[3,4,256]{2,1,0:T(4,128)S(1)} %bitcast.42) | data formatting | bytes 24576
Async XLA Ops:
  0.6 0.7 %copy-start.4 = (f32[256,16]{0,1:T(8,128)S(1)}, f32[256,16]{0,1:T(8,128)}, u32[]{:S(2)}) copy-start(f32[256,16]{0,1:T(8,128)} %param.15) | copy-start | bytes 49156
  0.6 0.7 %copy-start.6 = (s32[256]{0:T(256)S(1)}, s32[256]{0:T(256)}, u32[]{:S(2)}) copy-start(s32[256]{0:T(256)} %param.17) | copy-start | bytes 3076
  0.7 0.7 %copy-start.5 = (s32[256,1]{0,1:T(1,128)S(1)}, s32[256,1]{0,1:T(1,128)}, u32[]{:S(2)}) copy-start(s32[256,1]{0,1:T(1,128)} %param.16) | copy-start | bytes 3076
  0.7 0.7 %copy-start.7 = (f32[12]{0:T(128)S(1)}, f32[12]{0:T(128)}, u32[]{:S(2)}) copy-start(f32[12]{0:T(128)} %param.12) | copy-start | bytes 148
  1.4 1.0 %copy-start = (f32[16,4,1024]{2,1,0:T(4,128)S(1)}, f32[16,4,1024]{2,1,0:T(4,128)}, u32[]{:S(2)}) copy-start(f32[16,4,1024]{2,1,0:T(4,128)} %param.10) | copy-start | bytes 786436
  2.3 0.9 %copy-start.1 = (s32[16,4,1024]{2,1,0:T(4,128)S(1)}, s32[16,4,1024]{2,1,0:T(4,128)}, u32[]{:S(2)}) copy-start(s32[16,4,1024]{2,1,0:T(4,128)} %param.11) | copy-start | bytes 786436
  3.3 0.8 %copy-start.2 = (f32[3,4,1024]{2,1,0:T(4,128)S(1)}, f32[3,4,1024]{2,1,0:T(4,128)}, u32[]{:S(2)}) copy-start(f32[3,4,1024]{2,1,0:T(4,128)} %param.18) | copy-start | bytes 147460
  4.1 0.8 %copy-start.3 = (f32[3,4,1024]{2,1,0:T(4,128)S(1)}, f32[3,4,1024]{2,1,0:T(4,128)}, u32[]{:S(2)}) copy-start(f32[3,4,1024]{2,1,0:T(4,128)} %param.19) | copy-start | bytes 147460
  4.9 0.7 %copy-start.8 = (f32[12]{0:T(128)S(1)}, f32[12]{0:T(128)}, u32[]{:S(2)}) copy-start(f32[12]{0:T(128)} %param.13) | copy-start | bytes 148
  5.5 0.7 %copy-start.9 = (f32[12]{0:T(128)S(1)}, f32[12]{0:T(128)}, u32[]{:S(2)}) copy-start(f32[12]{0:T(128)} %param.14) | copy-start | bytes 148

commit v3 on v2

--- a/solution.py
+++ b/solution.py
@@ -630,7 +630,7 @@
             dma((2,)),
         ],
         compiler_params=pltpu.CompilerParams(
-            collective_id=0, has_side_effects=True, vmem_limit_bytes=32 * 1024 * 1024
+            collective_id=0, has_side_effects=True, vmem_limit_bytes=60 * 1024 * 1024
         ),
         name="coupled_step",
     )(

time: 36.5 us -> 32.2 us (0.88)
  local copies, waits for them, and re-layouts: 6.8 us -> 2.28 us
  Pallas kernels: 28.6 us -> 29.1 us
    unnamed x22 -> x4, local copies, waits for them, and re-layouts: 6.8 us -> 2.28 us
    pallas_call x1, Pallas kernels: 28.6 us -> 29.1 us  [body(): pl.pallas_call(functools.partial(kernel, wide_count, narrow_count), out_s...]
where the time goes in v3:
time: 32.2 us; the launch traced here: 32.1 us
  Pallas kernels  29.1 us (90%)
  local copies, waits for them, and re-layouts  2.28 us (7%)
  between operations  0.65 us (2%)
    pallas_call x1, Pallas kernels, body(): pl.pallas_call(functools.partial(kernel, wide_count, narrow_count), out_s...  29.1 us
    unnamed x4, local copies, waits for them, and re-layouts  2.28 us

profile of v3, /device:TPU:1, one launch (start us, length us, event | category | flops | bytes accessed | tf_op | source)
XLA Modules:
  0.0 32.1 jit_solution(2042205954746581370)
XLA Ops:
  0.6 29.1 %coupled_step.1 = (f32[512,128]{1,0:T(8,128)}, f32[24,128]{1,0:T(8,128)}) custom-call(f32[512,128]{1,0:T(8,128)} %bitcast.36, s32[512,128]{1,0:T(8,128)} %bitcast.37, f32[1,12]{1,0:T(1,128)} %bitcast.45, f32[1,12]{1,0:T(1,128)} %bitcast.46, f32[1,12]{1,0:T(1,128)} %bitcast.47, f32[16,256]{1,0:T(8,128)} %bitcast.41, s32[1,256]{1,0:T(1,128)} %bitcast.43, ...), custom_call_target="tpu_custom_call" | custom-call | tf_op jit(solution)/shard_map/coupled_step/pallas_call | solution.py:582
  29.8 0.0 copy-start
  29.8 1.7 %copy.20 = f32[16,4,1024]{2,1,0:T(4,128)} copy(f32[16,4,1024]{2,1,0:T(4,128)} %bitcast.38) | data formatting | bytes 524288
  31.5 0.0 copy-done
  31.5 0.6 %copy.21 = f32[3,4,256]{2,1,0:T(4,128)} copy(f32[3,4,256]{2,1,0:T(4,128)S(1)} %bitcast.42) | data formatting | bytes 24576
Async XLA Ops:
  29.8 1.7 %copy-start = (f32[24,128]{1,0:T(8,128)S(1)}, f32[24,128]{1,0:T(8,128)}, u32[]{:S(2)}) copy-start(f32[24,128]{1,0:T(8,128)} %get-tuple-element.5) | copy-start | bytes 36868

commit v4 on v3

--- a/solution.py
+++ b/solution.py
@@ -94,8 +94,10 @@
     column_hbm,
     aquifer_hbm,
     trans_hbm,
-    out_ref,
-    aquifer_out_ref,
+    stage_2,
+    part_hbm,
+    rest_hbm,
+    aquifer_next,
     head_ref,
     texture_ref,
     saturated_ref,
@@ -112,17 +114,17 @@
     part,
     face_out,
     face_in,
+    slab_in,
     slots,
     stage_1,
     turned,
-    stage_2,
     patch,
     patches,
     drain,
     drains,
     coef,
-    spread,
-    slot_lines,
+    aquifer_part,
+    store_done,
     load_done,
     slots_sent,
     slots_got,
@@ -255,19 +257,53 @@
 
     def conduct_layer(z, carry):
         here = pl.ds(pl.multiple_of(z * 32, 32), 32)
-        there = pl.ds(pl.multiple_of(z * 32 + 32, 32), 32)
         head = head_ref[here, :]
         index = texture_ref[here, :]
-        soil[0, there, :] = head
-        soil[1, there, :] = look_up(0, index) * jnp.exp(look_up(8, index) * jnp.minimum(head, 0.0))
+        soil[0, here, :] = head
+        soil[1, here, :] = look_up(0, index) * jnp.exp(look_up(8, index) * jnp.minimum(head, 0.0))
         rest[here, :] = TIME_STEP / look_up(16, index)
         return carry
 
-    lax.fori_loop(0, 16, conduct_layer, 0)
+    lax.fori_loop(0, 16, conduct_layer, 0, unroll=4)
+    rest_out = pltpu.make_async_copy(rest, rest_hbm, store_done.at[0])
+    rest_out.start()
+
+    for i, first in ((0, 3), (1, 0)):
+        for v in range(2):
+            face_out[i, v] = soil[v, pl.ds(first, 128, stride=4), :]
+    face_copies = [
+        send(
+            face_out.at[i],
+            face_in.at[i],
+            face_sent.at[i],
+            face_got.at[i],
+            wide_at(1 if i == 0 else -1),
+            n,
+        )
+        for i in range(2)
+    ]
+    slab_copies = [
+        send(
+            soil.at[:, pl.ds(480, 32)],
+            slab_in.at[0],
+            slab_sent.at[0],
+            slab_got.at[0],
+            w,
+            (n + 1) % narrow_count,
+        ),
+        send(
+            soil.at[:, pl.ds(0, 32)],
+            slab_in.at[1],
+            slab_sent.at[1],
+            slab_got.at[1],
+            w,
+            (n + narrow_count - 1) % narrow_count,
+        ),
+    ]
 
     @pl.when(bottom)
     def _():
-        flow = soil[1, 512:544, :] * (soil[0, 512:544, :] - aquifer_ref[0:32, :] + 1.0)
+        flow = soil[1, 480:512, :] * (soil[0, 480:512, :] - aquifer_ref[0:32, :] + 1.0)
         for q in range(4):
             drain[q, 0] = flow[8 * q : 8 * q + 4]
             drain[q, 1] = flow[8 * q + 4 : 8 * q + 8]
@@ -287,39 +323,6 @@
                     q,
                 )
         drains[:, 2] = drain[3]
-
-    for i, first in ((0, 35), (1, 32)):
-        for v in range(2):
-            face_out[i, v] = soil[v, pl.ds(first, 128, stride=4), :]
-    face_copies = [
-        send(
-            face_out.at[i],
-            face_in.at[i],
-            face_sent.at[i],
-            face_got.at[i],
-            wide_at(1 if i == 0 else -1),
-            n,
-        )
-        for i in range(2)
-    ]
-    slab_copies = [
-        send(
-            soil.at[:, pl.ds(512, 32)],
-            soil.at[:, pl.ds(0, 32)],
-            slab_sent.at[0],
-            slab_got.at[0],
-            w,
-            (n + 1) % narrow_count,
-        ),
-        send(
-            soil.at[:, pl.ds(32, 32)],
-            soil.at[:, pl.ds(544, 32)],
-            slab_sent.at[1],
-            slab_got.at[1],
-            w,
-            (n + narrow_count - 1) % narrow_count,
-        ),
-    ]
 
     for j in range(1, PEERS):
         other = (my_peer + PEERS - j) % PEERS
@@ -347,68 +350,62 @@
                 n,
             )
         )
-    stage_2[my_z] = turned[my_z]
-
-    for copy in slab_copies + face_copies:
-        copy.wait_recv()
-
-    @pl.when(n == 0)
-    def _():
-        soil[0, 0:32, :] = soil[0, 32:64, :]
-        soil[1, 0:32, :] = -soil[1, 32:64, :]
-
-    @pl.when(bottom)
-    def _():
-        soil[0, 544:576, :] = aquifer_ref[0:32, :]
-        soil[1, 544:576, :] = soil[1, 512:544, :]
+    own_rows = pltpu.make_async_copy(turned.at[my_z], stage_2.at[my_z], store_done.at[1])
+    own_rows.start()
 
     row = iota((32, 128), 0)
     lane = iota((32, 128), 1)
-    x = row % 4
-    sub8 = iota((8, 128), 0)
-    left_open = jnp.where((x == 0) & (w == 0), 0.0, 0.5)
-    right_open = jnp.where(w == wide_count - 1, 0.0, 0.5)
+    across_open = jnp.where(row % 4 == 0, 0.0, 0.5)
     along_open = jnp.where((lane == 0) & (row < 4), 0.0, 0.5)
-
-    def widened(side, v, z):
-        pieces = []
-        for j in range(4):
-            one = face_in[side, v, pl.ds(z * 8 + 2 * j, 1), :]
-            two = face_in[side, v, pl.ds(z * 8 + 2 * j + 1, 1), :]
-            pieces.append(
-                jnp.where(
-                    sub8 < 4, jnp.broadcast_to(one, (8, 128)), jnp.broadcast_to(two, (8, 128))
-                )
-            )
-        return jnp.concatenate(pieces, axis=0)
 
     def previous_column(v):
         moved = roll(v, 1, 1)
         return jnp.where(lane == 0, roll(moved, 4, 0), moved)
 
-    def balance_layer(z, carry):
-        over = pl.ds(pl.multiple_of(z * 32, 32), 32)
-        here = pl.ds(pl.multiple_of(z * 32 + 32, 32), 32)
-        under = pl.ds(pl.multiple_of(z * 32 + 64, 32), 32)
-        head, cond = soil[0, here, :], soil[1, here, :]
-        vertical_in = 0.5 * (soil[1, over, :] + cond) * (soil[0, over, :] - head + 1.0)
-        vertical_out = 0.5 * (cond + soil[1, under, :]) * (head - soil[0, under, :] + 1.0)
-        head_left = jnp.where(x == 0, widened(0, 0, z), roll(head, 1, 0))
-        cond_left = jnp.where(x == 0, widened(0, 1, z), roll(cond, 1, 0))
-        across_in = left_open * (cond_left + cond) * (head_left - head)
-        last = right_open * (cond + widened(1, 1, z)) * (head - widened(1, 0, z))
-        across_out = jnp.where(x == 3, last, roll(across_in, -1, 0))
-        along_in = along_open * (previous_column(cond) + cond) * (previous_column(head) - head)
-        moved = roll(along_in, -1, 1)
+    def layer(z):
+        at = pl.ds(pl.multiple_of(z * 32, 32), 32)
+        return soil[0, at, :], soil[1, at, :]
+
+    def sides(head, cond):
+        across = across_open * (roll(cond, 1, 0) + cond) * (roll(head, 1, 0) - head)
+        along = along_open * (previous_column(cond) + cond) * (previous_column(head) - head)
+        moved = roll(along, -1, 1)
         along_out = jnp.where(lane == 127, roll(moved, -4, 0), moved)
-        balance = (
-            (vertical_in - vertical_out) + (across_in - across_out) + (along_in - along_out)
-        )
+        return (across - roll(across, -1, 0)) + (along - along_out)
+
+    def balance_layer(z, vertical_in):
+        head, cond = layer(z)
+        head_under, cond_under = layer(z + 1)
+        vertical_out = 0.5 * (cond + cond_under) * (head - head_under + 1.0)
         at = pl.ds(pl.multiple_of(z * 32, 32), 32)
+        balance = (vertical_in - vertical_out) + sides(head, cond)
         part[at, :] = head + balance * rest[at, :]
-        return carry
-
-    lax.fori_loop(0, 16, balance_layer, 0)
+        return vertical_out
+
+    vertical_in = lax.fori_loop(0, 15, balance_layer, jnp.zeros((32, 128), F32), unroll=5)
+    head, cond = layer(15)
+    part[480:512, :] = head + (vertical_in + sides(head, cond)) * rest[480:512, :]
+
+    for copy in slab_copies + face_copies:
+        copy.wait_recv()
+    head_under = jnp.where(bottom, aquifer_ref[0:32, :], slab_in[1, 0])
+    cond_under = jnp.where(bottom, cond, slab_in[1, 1])
+    vertical_out = 0.5 * (cond + cond_under) * (head - head_under + 1.0)
+    part[480:512, :] = part[480:512, :] - vertical_out * rest[480:512, :]
+    head, cond = layer(0)
+    top_open = jnp.where(n == 0, 0.0, 0.5)
+    vertical_in = top_open * (slab_in[0, 1] + cond) * (slab_in[0, 0] - head + 1.0)
+    part[0:32, :] = part[0:32, :] + vertical_in * rest[0:32, :]
+    left_open = jnp.where(w == 0, 0.0, 0.5)
+    right_open = jnp.where(w == wide_count - 1, 0.0, -0.5)
+    for side, first, is_open in ((0, 0, left_open), (1, 3, right_open)):
+        head, cond = face_out[1 - side, 0], face_out[1 - side, 1]
+        other_head, other_cond = face_in[side, 0], face_in[side, 1]
+        jump = other_head - head if side == 0 else head - other_head
+        at = pl.ds(first, 128, stride=4)
+        part[at, :] = part[at, :] + is_open * (cond + other_cond) * jump * rest[at, :]
+    part_out = pltpu.make_async_copy(part, part_hbm, store_done.at[2])
+    part_out.start()
 
     for i, step in enumerate(around):
         pltpu.make_async_remote_copy(
@@ -495,9 +492,11 @@
 
     flat = lax.fori_loop(0, SWEEPS, sweep, tuple(v for layer in heads for v in layer))
     for l in range(3):
-        aquifer_out_ref[8 * l : 8 * l + 8, :] = jnp.concatenate(
+        aquifer_part[8 * l : 8 * l + 8, :] = jnp.concatenate(
             [flat[3 * l][8:12], flat[3 * l + 1][8:12]], axis=0
         )
+    aquifer_out = pltpu.make_async_copy(aquifer_part, aquifer_next, store_done.at[3])
+    aquifer_out.start()
 
     for j in range(1, depth):
         other = (my_z + depth - j) % depth
@@ -509,32 +508,8 @@
             device_id=(w, n),
             device_id_type=MESH,
         ).wait_recv()
-    slot_lines[...] = stage_2[...].reshape(128, 128).T
-    lanes = iota((128, 128), 0).astype(F32)
-    rows = iota((32, 128), 0).astype(F32)
-    target = jnp.concatenate(
-        [
-            (lanes == slot_lines[32 * k + 17 : 32 * k + 18, :]).astype(F32).astype(BF16)
-            for k in range(CAP)
-        ],
-        axis=1,
-    )
-    for k in range(CAP):
-        hit = rows == slot_lines[32 * k + 16 : 32 * k + 17, :]
-
-        def place(z, carry, k=k, hit=hit):
-            value = slot_lines[pl.ds(32 * k + z, 1), :]
-            value = jnp.where(hit, jnp.broadcast_to(value, (32, 128)), 0.0)
-            high = value.astype(BF16)
-            low = (value - high.astype(F32)).astype(BF16)
-            spread[pl.ds(pl.multiple_of(z * 32, 32), 32), 128 * k : 128 * k + 128] = high
-            spread[pl.ds(pl.multiple_of(z * 32 + 512, 32), 32), 128 * k : 128 * k + 128] = low
-            return carry
-
-        lax.fori_loop(0, 16, place, 0)
-    taken = lax.dot_general(spread[...], target, NT, preferred_element_type=F32)
-    out_ref[...] = part[...] - (taken[:512] + taken[512:]) * rest[...]
-
+    for copy in (rest_out, own_rows, part_out, aquifer_out):
+        copy.wait()
     for copy in first_stage + patch_copies + face_copies + slab_copies + second_stage:
         copy.wait_send()
 
@@ -552,6 +527,59 @@
                     device_id=(w, n),
                     device_id_type=MESH,
                 ).wait_send()
+
+
+def finish(
+    rows_hbm,
+    part_hbm,
+    rest_hbm,
+    aquifer_hbm,
+    out_hbm,
+    aquifer_out_hbm,
+    rows_in,
+    part,
+    rest,
+    out,
+    spread,
+    slot_lines,
+    done,
+):
+    pairs = ((rows_hbm, rows_in), (part_hbm, part), (rest_hbm, rest), (aquifer_hbm, aquifer_out_hbm))
+    loads = [pltpu.make_async_copy(a, b, done.at[i]) for i, (a, b) in enumerate(pairs)]
+    for load in loads:
+        load.start()
+    loads[0].wait()
+    slot_lines[...] = rows_in[...].T
+    lanes = iota((128, 128), 0).astype(F32)
+    rows = iota((32, 128), 0).astype(F32)
+    target = jnp.concatenate(
+        [
+            (lanes == slot_lines[32 * k + 17 : 32 * k + 18, :]).astype(F32).astype(BF16)
+            for k in range(CAP)
+        ],
+        axis=1,
+    )
+    for k in range(CAP):
+        hit = rows == slot_lines[32 * k + 16 : 32 * k + 17, :]
+
+        def place(z, carry, k=k, hit=hit):
+            value = slot_lines[pl.ds(32 * k + z, 1), :]
+            value = jnp.where(hit, jnp.broadcast_to(value, (32, 128)), 0.0)
+            high = value.astype(BF16)
+            low = (value - high.astype(F32)).astype(BF16)
+            spread[pl.ds(pl.multiple_of(z * 32, 32), 32), 128 * k : 128 * k + 128] = high
+            spread[pl.ds(pl.multiple_of(z * 32 + 512, 32), 32), 128 * k : 128 * k + 128] = low
+            return carry
+
+        lax.fori_loop(0, 16, place, 0, unroll=4)
+    taken = lax.dot_general(spread[...], target, NT, preferred_element_type=F32)
+    loads[1].wait()
+    loads[2].wait()
+    out[...] = part[...] - (taken[:512] + taken[512:]) * rest[...]
+    stored = pltpu.make_async_copy(out, out_hbm, done.at[4])
+    stored.start()
+    loads[3].wait()
+    stored.wait()
 
 
 def rows_of(a):
@@ -579,14 +607,17 @@
     narrow_count = lax.axis_size("narrow")
     depth = wide_count // PEERS
     dma = pltpu.SemaphoreType.DMA
-    out, aquifer_out = pl.pallas_call(
+    hbm = pl.BlockSpec(memory_space=pl.ANY)
+    rows_in, part, rest, aquifer_next = pl.pallas_call(
         functools.partial(kernel, wide_count, narrow_count),
         out_shape=(
+            jax.ShapeDtypeStruct((depth, PEERS, 128), F32),
+            jax.ShapeDtypeStruct((512, 128), F32),
             jax.ShapeDtypeStruct((512, 128), F32),
             jax.ShapeDtypeStruct((24, 128), F32),
         ),
-        in_specs=[pl.BlockSpec(memory_space=pltpu.HBM)] * 10,
-        out_specs=[pl.BlockSpec(memory_space=pltpu.VMEM)] * 2,
+        in_specs=[hbm] * 10,
+        out_specs=[hbm] * 4,
         scratch_shapes=[
             pltpu.VMEM((512, 128), F32),
             pltpu.VMEM((512, 128), I32),
@@ -599,22 +630,22 @@
             pltpu.VMEM((96, 128), F32),
             pltpu.VMEM((96, 128), F32),
             pltpu.VMEM((24, 128), F32),
-            pltpu.VMEM((2, 576, 128), F32),
+            pltpu.VMEM((2, 512, 128), F32),
             pltpu.VMEM((512, 128), F32),
             pltpu.VMEM((512, 128), F32),
             pltpu.VMEM((2, 2, 128, 128), F32),
             pltpu.VMEM((2, 2, 128, 128), F32),
+            pltpu.VMEM((2, 2, 32, 128), F32),
             pltpu.VMEM((PEERS, depth, 128), F32),
             pltpu.VMEM((PEERS, depth, 128), F32),
-            pltpu.VMEM((depth, PEERS, 128), F32),
             pltpu.VMEM((depth, PEERS, 128), F32),
             pltpu.VMEM((18, 4, 128), F32),
             pltpu.VMEM((18, 6, 4, 128), F32),
             pltpu.VMEM((4, 3, 4, 128), F32),
             pltpu.VMEM((3, 6, 4, 128), F32),
             pltpu.VMEM((6, 9, 24, 128), F32),
-            pltpu.VMEM((1024, 512), BF16),
-            pltpu.VMEM((128, 128), F32),
+            pltpu.VMEM((24, 128), F32),
+            dma((4,)),
             dma((10,)),
             dma((PEERS,)),
             dma((PEERS,)),
@@ -645,6 +676,26 @@
         rows_of(aquifer_head),
         rows_of(transmissivity),
     )
+    out, aquifer_out = pl.pallas_call(
+        finish,
+        out_shape=(
+            jax.ShapeDtypeStruct((512, 128), F32),
+            jax.ShapeDtypeStruct((24, 128), F32),
+        ),
+        in_specs=[hbm] * 4,
+        out_specs=[hbm] * 2,
+        scratch_shapes=[
+            pltpu.VMEM((128, 128), F32),
+            pltpu.VMEM((512, 128), F32),
+            pltpu.VMEM((512, 128), F32),
+            pltpu.VMEM((512, 128), F32),
+            pltpu.VMEM((1024, 512), BF16),
+            pltpu.VMEM((128, 128), F32),
+            dma((5,)),
+        ],
+        compiler_params=pltpu.CompilerParams(vmem_limit_bytes=60 * 1024 * 1024),
+        name="finish_step",
+    )(rows_in.reshape(128, 128), part, rest, aquifer_next)
     return grid_of(out, 16, 1024), grid_of(aquifer_out, 3, 256)
 
 

time: 32.2 us -> 32.1 us (level)
  local copies, waits for them, and re-layouts: 2.28 us -> 0 us
  Pallas kernels: 29.1 us -> 31.3 us
    pallas_call x0 -> x1, Pallas kernels: none -> 2.46 us  [body(): pl.pallas_call(finish, out_shape=(jax.ShapeDtypeStruct((512, 128), F32),...]
    unnamed x4 -> x0, local copies, waits for them, and re-layouts: 2.28 us -> none
where the time goes in v4:
time: 32.1 us; the launch traced here: 32 us
  Pallas kernels  31.3 us (98%)
  between operations  0.64 us (2%)
    pallas_call x1, Pallas kernels, body(): pl.pallas_call(functools.partial(kernel, wide_count, narrow_count), out_s...  28.9 us
    pallas_call x1, Pallas kernels, body(): pl.pallas_call(finish, out_shape=(jax.ShapeDtypeStruct((512, 128), F32),...  2.46 us

profile of v4, /device:TPU:1, one launch (start us, length us, event | category | flops | bytes accessed | tf_op | source)
XLA Modules:
  0.0 32.0 jit_solution(17647978007183761518)
XLA Ops:
  0.6 28.9 %coupled_step.1 = (f32[16,8,128]{2,1,0:T(8,128)}, f32[512,128]{1,0:T(8,128)}, f32[512,128]{1,0:T(8,128)}, f32[24,128]{1,0:T(8,128)}) custom-call(f32[512,128]{1,0:T(8,128)} %bitcast.37, s32[512,128]{1,0:T(8,128)} %bitcast.38, f32[1,12]{1,0:T(1,128)} %bitcast.45, f32[1,12]{1,0:T(1,128)} %bitcast.46, f32[1,12]{1,0:T(1,128)} %bitcast.47, f32[16,256]{1,0:T(8,128)} %bitcast.42, ...), custom_call_target="tpu_custom_call" | custom-call | tf_op jit(solution)/shard_map/coupled_step/pallas_call | solution.py:611
  29.5 2.5 %finish_step.1 = (f32[512,128]{1,0:T(8,128)}, f32[24,128]{1,0:T(8,128)}) custom-call(f32[128,128]{1,0:T(8,128)} %bitcast.39, f32[512,128]{1,0:T(8,128)} %get-tuple-element.9.part_hbm, f32[512,128]{1,0:T(8,128)} %get-tuple-element.10.rest_hbm, f32[24,128]{1,0:T(8,128)} %get-tuple-element.11.aquifer_hbm), custom_call_target="tpu_custom_call" | custom-call | tf_op jit(solution)/shard_map/finish_step/pallas_call | solution.py:679

commit v5 on v4

--- a/solution.py
+++ b/solution.py
@@ -39,12 +39,11 @@
     return copy
 
 
-def root_slots(uptake, tile, column, order):
-    place = order(tile)
+def root_slots(uptake, tile, column):
     cell_row = ((column // 128) % 8) * 4 + column // 1024
     cell_lane = column % 128
     count = tile.shape[1]
-    aimed = iota((128, count), 0) == place
+    aimed = iota((128, count), 0) == tile
     earlier = iota((count, count), 0) < iota((count, count), 1)
     rank = jnp.dot(
         aimed.astype(F32).astype(BF16),
@@ -94,7 +93,7 @@
     column_hbm,
     aquifer_hbm,
     trans_hbm,
-    stage_2,
+    rows,
     part_hbm,
     rest_hbm,
     aquifer_next,
@@ -116,8 +115,6 @@
     face_in,
     slab_in,
     slots,
-    stage_1,
-    turned,
     patch,
     patches,
     drain,
@@ -126,10 +123,8 @@
     aquifer_part,
     store_done,
     load_done,
-    slots_sent,
-    slots_got,
-    turned_sent,
-    turned_got,
+    rows_sent,
+    rows_got,
     patch_sent,
     patch_got,
     drain_sent,
@@ -163,14 +158,28 @@
     def greet(wide, narrow):
         pl.semaphore_signal(barrier, inc=1, device_id=(wide, narrow), device_id_type=MESH)
 
-    for j in range(1, PEERS):
-        greet(my_z * PEERS + (my_peer + j) % PEERS, n)
-    for j in range(1, depth):
-        greet(((my_z + j) % depth) * PEERS + my_peer, n)
+    peers = [(my_peer + j) % PEERS for j in range(1, PEERS + 1)]
+
+    def greet_plane(z, carry):
+        for peer in peers:
+            greet(z * PEERS + peer, n)
+        return carry
+
+    lax.fori_loop(my_z + 1, depth, greet_plane, 0)
+    for peer in peers[:-1]:
+        greet(my_z * PEERS + peer, n)
+    later_around = 0
     for step in around:
-        greet(wide_at(step), n)
+        plane = wide_at(step) // PEERS
+        later_around = later_around + jnp.where(plane > my_z, 1, 0)
+
+        @pl.when(plane < my_z)
+        def _(step=step):
+            greet(wide_at(step), n)
+
     greet(w, (n + 1) % narrow_count)
     greet(w, (n + narrow_count - 1) % narrow_count)
+    greeted = PEERS * my_z + PEERS - 1 + later_around + 2
 
     @pl.when(jnp.logical_not(bottom))
     def _():
@@ -184,9 +193,8 @@
         uptake_ref[...],
         tile_ref[...],
         column_ref[...],
-        lambda tile: (tile % PEERS) * depth + tile // PEERS,
     )
-    slots[...] = made.reshape(PEERS, depth, 128)
+    slots[...] = made
 
     for i in (8, 9):
         loads[i].wait()
@@ -210,26 +218,43 @@
 
     @pl.when(bottom)
     def _():
-        pl.semaphore_wait(barrier, PEERS - 1 + depth - 1 + 6 + 5 * (narrow_count - 1))
+        pl.semaphore_wait(barrier, greeted + 5 * (narrow_count - 1))
 
     @pl.when(jnp.logical_not(bottom))
     def _():
-        pl.semaphore_wait(barrier, PEERS - 1 + depth - 1 + 6)
-
-    first_stage = []
-    for j in range(1, PEERS):
-        peer = (my_peer + j) % PEERS
-        first_stage.append(
-            send(
-                slots.at[peer],
-                stage_1.at[my_peer],
-                slots_sent.at[j],
-                slots_got.at[j],
-                my_z * PEERS + peer,
-                n,
-            )
+        pl.semaphore_wait(barrier, greeted)
+
+    def send_rows(tile):
+        pltpu.make_async_remote_copy(
+            src_ref=slots.at[pl.ds(tile, 1)],
+            dst_ref=rows.at[w],
+            send_sem=rows_sent.at[0],
+            recv_sem=rows_got.at[my_z],
+            device_id=(tile, n),
+            device_id_type=MESH,
+        ).start()
+
+    def rows_from(first, count, sent, got):
+        at = pl.ds(first, count)
+        return pltpu.make_async_remote_copy(
+            src_ref=rows.at[at],
+            dst_ref=rows.at[at],
+            send_sem=sent,
+            recv_sem=got,
+            device_id=(w, n),
+            device_id_type=MESH,
         )
-    stage_1[my_peer] = slots[my_peer]
+
+    def send_plane(z, carry):
+        for peer in peers:
+            send_rows(z * PEERS + peer)
+        return carry
+
+    lax.fori_loop(0, my_z, send_plane, 0)
+    for peer in peers[:-1]:
+        send_rows(my_z * PEERS + peer)
+    own_rows = pltpu.make_async_copy(slots.at[pl.ds(w, 1)], rows.at[w], store_done.at[1])
+    own_rows.start()
 
     patch_copies = []
     for i, step in enumerate(around):
@@ -324,35 +349,6 @@
                 )
         drains[:, 2] = drain[3]
 
-    for j in range(1, PEERS):
-        other = (my_peer + PEERS - j) % PEERS
-        pltpu.make_async_remote_copy(
-            src_ref=slots.at[other],
-            dst_ref=stage_1.at[other],
-            send_sem=slots_sent.at[j],
-            recv_sem=slots_got.at[j],
-            device_id=(w, n),
-            device_id_type=MESH,
-        ).wait_recv()
-    for z in range(depth):
-        for p in range(PEERS):
-            turned[z, p : p + 1] = stage_1[p, z : z + 1]
-    second_stage = []
-    for j in range(1, depth):
-        other = (my_z + j) % depth
-        second_stage.append(
-            send(
-                turned.at[other],
-                stage_2.at[my_z],
-                turned_sent.at[j],
-                turned_got.at[j],
-                other * PEERS + my_peer,
-                n,
-            )
-        )
-    own_rows = pltpu.make_async_copy(turned.at[my_z], stage_2.at[my_z], store_done.at[1])
-    own_rows.start()
-
     row = iota((32, 128), 0)
     lane = iota((32, 128), 1)
     across_open = jnp.where(row % 4 == 0, 0.0, 0.5)
@@ -498,20 +494,23 @@
     aquifer_out = pltpu.make_async_copy(aquifer_part, aquifer_next, store_done.at[3])
     aquifer_out.start()
 
-    for j in range(1, depth):
-        other = (my_z + depth - j) % depth
-        pltpu.make_async_remote_copy(
-            src_ref=turned.at[other],
-            dst_ref=stage_2.at[other],
-            send_sem=turned_sent.at[j],
-            recv_sem=turned_got.at[j],
-            device_id=(w, n),
-            device_id_type=MESH,
-        ).wait_recv()
+    def answer_plane(z, carry):
+        rows_from(0, PEERS, rows_sent.at[0], rows_got.at[z]).wait_recv()
+        return send_plane(z, carry)
+
+    def await_plane(z, carry):
+        rows_from(0, PEERS, rows_sent.at[0], rows_got.at[z]).wait_recv()
+        return carry
+
+    lax.fori_loop(my_z + 1, depth, answer_plane, 0)
+    rows_from(0, PEERS - 1, rows_sent.at[0], rows_got.at[my_z]).wait_recv()
+    lax.fori_loop(0, my_z, await_plane, 0)
+
     for copy in (rest_out, own_rows, part_out, aquifer_out):
         copy.wait()
-    for copy in first_stage + patch_copies + face_copies + slab_copies + second_stage:
+    for copy in patch_copies + face_copies + slab_copies:
         copy.wait_send()
+    rows_from(0, wide_count - 1, rows_sent.at[0], rows_got.at[0]).wait_send()
 
     @pl.when(bottom)
     def _():
@@ -611,7 +610,7 @@
     rows_in, part, rest, aquifer_next = pl.pallas_call(
         functools.partial(kernel, wide_count, narrow_count),
         out_shape=(
-            jax.ShapeDtypeStruct((depth, PEERS, 128), F32),
+            jax.ShapeDtypeStruct((wide_count, 1, 128), F32),
             jax.ShapeDtypeStruct((512, 128), F32),
             jax.ShapeDtypeStruct((512, 128), F32),
             jax.ShapeDtypeStruct((24, 128), F32),
@@ -636,9 +635,7 @@
             pltpu.VMEM((2, 2, 128, 128), F32),
             pltpu.VMEM((2, 2, 128, 128), F32),
             pltpu.VMEM((2, 2, 32, 128), F32),
-            pltpu.VMEM((PEERS, depth, 128), F32),
-            pltpu.VMEM((PEERS, depth, 128), F32),
-            pltpu.VMEM((depth, PEERS, 128), F32),
+            pltpu.VMEM((wide_count, 128), F32),
             pltpu.VMEM((18, 4, 128), F32),
             pltpu.VMEM((18, 6, 4, 128), F32),
             pltpu.VMEM((4, 3, 4, 128), F32),
@@ -647,9 +644,7 @@
             pltpu.VMEM((24, 128), F32),
             dma((4,)),
             dma((10,)),
-            dma((PEERS,)),
-            dma((PEERS,)),
-            dma((depth,)),
+            dma((1,)),
             dma((depth,)),
             dma((4,)),
             dma((4,)),

time: 32.1 us -> 35.4 us (1.10)
  Pallas kernels: 31.3 us -> 34.6 us
    pallas_call x1, Pallas kernels: 28.9 us -> 32.2 us  [body(): pl.pallas_call(functools.partial(kernel, wide_count, narrow_count), out_s...]
where the time goes in v5:
time: 35.4 us; the launch traced here: 35.3 us
  Pallas kernels  34.6 us (98%)
  between operations  0.64 us (2%)
    pallas_call x1, Pallas kernels, body(): pl.pallas_call(functools.partial(kernel, wide_count, narrow_count), out_s...  32.2 us
    pallas_call x1, Pallas kernels, body(): pl.pallas_call(finish, out_shape=(jax.ShapeDtypeStruct((512, 128), F32),...  2.47 us

profile of v5, /device:TPU:1, one launch (start us, length us, event | category | flops | bytes accessed | tf_op | source)
XLA Modules:
  0.0 35.3 jit_solution(8042482314616221110)
XLA Ops:
  0.6 32.2 %coupled_step.1 = (f32[128,1,128]{2,1,0:T(1,128)}, f32[512,128]{1,0:T(8,128)}, f32[512,128]{1,0:T(8,128)}, f32[24,128]{1,0:T(8,128)}) custom-call(f32[512,128]{1,0:T(8,128)} %bitcast.37, s32[512,128]{1,0:T(8,128)} %bitcast.38, f32[1,12]{1,0:T(1,128)} %bitcast.45, f32[1,12]{1,0:T(1,128)} %bitcast.46, f32[1,12]{1,0:T(1,128)} %bitcast.47, f32[16,256]{1,0:T(8,128)} %bitcast.42, ...), custom_call_target="tpu_custom_call" | custom-call | tf_op jit(solution)/shard_map/coupled_step/pallas_call | solution.py:610
  32.8 2.5 %finish_step.1 = (f32[512,128]{1,0:T(8,128)}, f32[24,128]{1,0:T(8,128)}) custom-call(f32[128,128]{1,0:T(8,128)} %bitcast.39, f32[512,128]{1,0:T(8,128)} %get-tuple-element.9.part_hbm, f32[512,128]{1,0:T(8,128)} %get-tuple-element.10.rest_hbm, f32[24,128]{1,0:T(8,128)} %get-tuple-element.11.aquifer_hbm), custom_call_target="tpu_custom_call" | custom-call | tf_op jit(solution)/shard_map/finish_step/pallas_call | solution.py:674

commit v6 on v5

--- a/solution.py
+++ b/solution.py
@@ -26,8 +26,8 @@
     return lax.broadcasted_iota(I32, shape, axis)
 
 
-def send(src, dst, send_sem, recv_sem, wide, narrow):
-    copy = pltpu.make_async_remote_copy(
+def remote(src, dst, send_sem, recv_sem, wide, narrow):
+    return pltpu.make_async_remote_copy(
         src_ref=src,
         dst_ref=dst,
         send_sem=send_sem,
@@ -35,8 +35,6 @@
         device_id=(wide, narrow),
         device_id_type=MESH,
     )
-    copy.start()
-    return copy
 
 
 def root_slots(uptake, tile, column):
@@ -141,10 +139,43 @@
     bottom = n == narrow_count - 1
     around = (-2, -1, 1, 2)
 
-    def wide_at(step):
-        return (w + step + wide_count) % wide_count
-
-    order = (6, 7, 5, 8, 9, 0, 1, 2, 3, 4)
+    def exists(step):
+        return (w + step >= 0) & (w + step < wide_count)
+
+    barrier = pltpu.get_barrier_semaphore()
+
+    def greet(wide, narrow):
+        pl.semaphore_signal(barrier, inc=1, device_id=(wide, narrow), device_id_type=MESH)
+
+    peers = [(my_peer + j) % PEERS for j in range(1, PEERS + 1)]
+
+    def greet_plane(z, carry):
+        for peer in peers:
+            greet(z * PEERS + peer, n)
+        return carry
+
+    lax.fori_loop(my_z + 1, depth, greet_plane, 0)
+    for peer in peers[:-1]:
+        greet(my_z * PEERS + peer, n)
+    greeted = PEERS * my_z + PEERS - 1 + 2
+    for step in around:
+        plane = (w + step + PEERS) // PEERS - 1
+        greeted = greeted + jnp.where(exists(step) & (plane > my_z), 1, 0)
+
+        @pl.when(exists(step) & (plane < my_z))
+        def _(step=step):
+            greet(w + step, n)
+
+    greet(w, (n + 1) % narrow_count)
+    greet(w, (n + narrow_count - 1) % narrow_count)
+
+    for step in (-2, -1, 0, 1, 2):
+
+        @pl.when(jnp.logical_not(bottom) & exists(step))
+        def _(step=step):
+            greet(w + step, narrow_count - 1)
+
+    order = (6, 7, 5, 0, 1, 2, 3, 4, 8, 9)
     held = (head_ref, texture_ref, saturated_ref, shape_ref, capacity_ref, uptake_ref, tile_ref)
     held += (column_ref, aquifer_ref, trans_ref)
     far = (head_hbm, texture_hbm, saturated_hbm, shape_hbm, capacity_hbm, uptake_hbm, tile_hbm)
@@ -152,40 +183,6 @@
     loads = [pltpu.make_async_copy(far[i], held[i], load_done.at[i]) for i in range(10)]
     for i in order:
         loads[i].start()
-
-    barrier = pltpu.get_barrier_semaphore()
-
-    def greet(wide, narrow):
-        pl.semaphore_signal(barrier, inc=1, device_id=(wide, narrow), device_id_type=MESH)
-
-    peers = [(my_peer + j) % PEERS for j in range(1, PEERS + 1)]
-
-    def greet_plane(z, carry):
-        for peer in peers:
-            greet(z * PEERS + peer, n)
-        return carry
-
-    lax.fori_loop(my_z + 1, depth, greet_plane, 0)
-    for peer in peers[:-1]:
-        greet(my_z * PEERS + peer, n)
-    later_around = 0
-    for step in around:
-        plane = wide_at(step) // PEERS
-        later_around = later_around + jnp.where(plane > my_z, 1, 0)
-
-        @pl.when(plane < my_z)
-        def _(step=step):
-            greet(wide_at(step), n)
-
-    greet(w, (n + 1) % narrow_count)
-    greet(w, (n + narrow_count - 1) % narrow_count)
-    greeted = PEERS * my_z + PEERS - 1 + later_around + 2
-
-    @pl.when(jnp.logical_not(bottom))
-    def _():
-        for step in (-2, -1, 0, 1, 2):
-            greet(wide_at(step), narrow_count - 1)
-
     for i in (6, 7, 5):
         loads[i].wait()
 
@@ -216,59 +213,6 @@
     for t in range(3):
         drains[t, 5] = jnp.zeros((4, 128), F32)
 
-    @pl.when(bottom)
-    def _():
-        pl.semaphore_wait(barrier, greeted + 5 * (narrow_count - 1))
-
-    @pl.when(jnp.logical_not(bottom))
-    def _():
-        pl.semaphore_wait(barrier, greeted)
-
-    def send_rows(tile):
-        pltpu.make_async_remote_copy(
-            src_ref=slots.at[pl.ds(tile, 1)],
-            dst_ref=rows.at[w],
-            send_sem=rows_sent.at[0],
-            recv_sem=rows_got.at[my_z],
-            device_id=(tile, n),
-            device_id_type=MESH,
-        ).start()
-
-    def rows_from(first, count, sent, got):
-        at = pl.ds(first, count)
-        return pltpu.make_async_remote_copy(
-            src_ref=rows.at[at],
-            dst_ref=rows.at[at],
-            send_sem=sent,
-            recv_sem=got,
-            device_id=(w, n),
-            device_id_type=MESH,
-        )
-
-    def send_plane(z, carry):
-        for peer in peers:
-            send_rows(z * PEERS + peer)
-        return carry
-
-    lax.fori_loop(0, my_z, send_plane, 0)
-    for peer in peers[:-1]:
-        send_rows(my_z * PEERS + peer)
-    own_rows = pltpu.make_async_copy(slots.at[pl.ds(w, 1)], rows.at[w], store_done.at[1])
-    own_rows.start()
-
-    patch_copies = []
-    for i, step in enumerate(around):
-        patch_copies.append(
-            send(
-                patch,
-                patches.at[:, 2 - step],
-                patch_sent.at[i],
-                patch_got.at[i],
-                wide_at(step),
-                n,
-            )
-        )
-
     for i in (0, 1, 2, 3, 4):
         loads[i].wait()
     table[...] = jnp.zeros_like(table)
@@ -296,36 +240,6 @@
     for i, first in ((0, 3), (1, 0)):
         for v in range(2):
             face_out[i, v] = soil[v, pl.ds(first, 128, stride=4), :]
-    face_copies = [
-        send(
-            face_out.at[i],
-            face_in.at[i],
-            face_sent.at[i],
-            face_got.at[i],
-            wide_at(1 if i == 0 else -1),
-            n,
-        )
-        for i in range(2)
-    ]
-    slab_copies = [
-        send(
-            soil.at[:, pl.ds(480, 32)],
-            slab_in.at[0],
-            slab_sent.at[0],
-            slab_got.at[0],
-            w,
-            (n + 1) % narrow_count,
-        ),
-        send(
-            soil.at[:, pl.ds(0, 32)],
-            slab_in.at[1],
-            slab_sent.at[1],
-            slab_got.at[1],
-            w,
-            (n + narrow_count - 1) % narrow_count,
-        ),
-    ]
-
     @pl.when(bottom)
     def _():
         flow = soil[1, 480:512, :] * (soil[0, 480:512, :] - aquifer_ref[0:32, :] + 1.0)
@@ -335,19 +249,88 @@
             after = flow[8 * q + 8 : 8 * q + 12] if q < 3 else jnp.zeros((4, 128), F32)
             before = flow[8 * q - 4 : 8 * q] if q > 0 else jnp.zeros((4, 128), F32)
             drain[q, 2] = jnp.where(lane4 < 64, after, before)
+        drains[:, 2] = drain[3]
+
+    near_tiles = sum(jnp.where(exists(step), 1, 0) for step in (-2, -1, 0, 1, 2))
+    greeted = greeted + jnp.where(bottom, (narrow_count - 1) * near_tiles, 0)
+    pl.semaphore_wait(barrier, greeted)
+
+    def send_rows(tile):
+        remote(
+            slots.at[pl.ds(tile, 1)], rows.at[w], rows_sent.at[0], rows_got.at[my_z], tile, n
+        ).start()
+
+    def rows_from(count, z):
+        at = rows.at[pl.ds(0, count)]
+        return remote(at, at, rows_sent.at[0], rows_got.at[z], w, n)
+
+    def send_plane(z, carry):
+        for peer in peers:
+            send_rows(z * PEERS + peer)
+        return carry
+
+    lax.fori_loop(0, my_z, send_plane, 0)
+    for peer in peers[:-1]:
+        send_rows(my_z * PEERS + peer)
+    own_rows = pltpu.make_async_copy(slots.at[pl.ds(w, 1)], rows.at[w], store_done.at[1])
+    own_rows.start()
+
+    def answer_plane(z, carry):
+        rows_from(PEERS, z).wait_recv()
+        return send_plane(z, carry)
+
+    def await_plane(z, carry):
+        rows_from(PEERS, z).wait_recv()
+        return carry
+
+    face_copies = [
+        remote(face_out.at[i], face_in.at[i], face_sent.at[i], face_got.at[i], w + step, n)
+        for i, step in ((0, 1), (1, -1))
+    ]
+    for copy, step in zip(face_copies, (1, -1)):
+        pl.when(exists(step))(copy.start)
+    slab_copies = [
+        remote(
+            soil.at[:, pl.ds(first, 32)],
+            slab_in.at[i],
+            slab_sent.at[i],
+            slab_got.at[i],
+            w,
+            (n + step) % narrow_count,
+        )
+        for i, first, step in ((0, 480, 1), (1, 0, narrow_count - 1))
+    ]
+    for copy in slab_copies:
+        copy.start()
+    patch_copies = [
+        remote(patch, patches.at[:, 2 - step], patch_sent.at[i], patch_got.at[i], w + step, n)
+        for i, step in enumerate(around)
+    ]
+    for copy, step in zip(patch_copies, around):
+        pl.when(exists(step))(copy.start)
+
+    def drain_copy(step, q):
+        return remote(
+            drain.at[q],
+            drains.at[:, 2 - step],
+            drain_sent.at[step + 2, q],
+            drain_got.at[2 - step],
+            w + step,
+            q,
+        )
+
+    def each_drain(act):
         for step in (0, 1, -1, 2, -2):
-            for q in range(4):
-                if step == 0 and q == 3:
-                    continue
-                send(
-                    drain.at[q],
-                    drains.at[:, 2 - step],
-                    drain_sent.at[step + 2, q],
-                    drain_got.at[2 - step],
-                    wide_at(step),
-                    q,
-                )
-        drains[:, 2] = drain[3]
+
+            @pl.when(bottom & exists(step))
+            def _(step=step):
+                for q in range(narrow_count - 1 if step == 0 else narrow_count):
+                    act(drain_copy(step, q))
+
+    each_drain(lambda copy: copy.start())
+
+    def answer():
+        lax.fori_loop(my_z + 1, depth, answer_plane, 0)
 
     row = iota((32, 128), 0)
     lane = iota((32, 128), 1)
@@ -382,8 +365,12 @@
     head, cond = layer(15)
     part[480:512, :] = head + (vertical_in + sides(head, cond)) * rest[480:512, :]
 
-    for copy in slab_copies + face_copies:
+    pl.when(my_z >= depth // 2)(answer)
+
+    for copy in slab_copies:
         copy.wait_recv()
+    for copy, step in zip(face_copies, (1, -1)):
+        pl.when(exists(-step))(copy.wait_recv)
     head_under = jnp.where(bottom, aquifer_ref[0:32, :], slab_in[1, 0])
     cond_under = jnp.where(bottom, cond, slab_in[1, 1])
     vertical_out = 0.5 * (cond + cond_under) * (head - head_under + 1.0)
@@ -392,57 +379,37 @@
     top_open = jnp.where(n == 0, 0.0, 0.5)
     vertical_in = top_open * (slab_in[0, 1] + cond) * (slab_in[0, 0] - head + 1.0)
     part[0:32, :] = part[0:32, :] + vertical_in * rest[0:32, :]
-    left_open = jnp.where(w == 0, 0.0, 0.5)
-    right_open = jnp.where(w == wide_count - 1, 0.0, -0.5)
-    for side, first, is_open in ((0, 0, left_open), (1, 3, right_open)):
+    for side, first, factor, is_open in ((0, 0, 0.5, exists(-1)), (1, 3, -0.5, exists(1))):
         head, cond = face_out[1 - side, 0], face_out[1 - side, 1]
         other_head, other_cond = face_in[side, 0], face_in[side, 1]
         jump = other_head - head if side == 0 else head - other_head
         at = pl.ds(first, 128, stride=4)
-        part[at, :] = part[at, :] + is_open * (cond + other_cond) * jump * rest[at, :]
+        flow = jnp.where(is_open, factor * (cond + other_cond) * jump, 0.0)
+        part[at, :] = part[at, :] + flow * rest[at, :]
     part_out = pltpu.make_async_copy(part, part_hbm, store_done.at[2])
     part_out.start()
 
-    for i, step in enumerate(around):
-        pltpu.make_async_remote_copy(
-            src_ref=patch,
-            dst_ref=patches.at[:, 2 - step],
-            send_sem=patch_sent.at[i],
-            recv_sem=patch_got.at[i],
-            device_id=(w, n),
-            device_id_type=MESH,
-        ).wait_recv()
+    for copy, step in zip(patch_copies, around):
+        pl.when(exists(-step))(copy.wait_recv)
     for step in (-2, -1, 0, 1, 2):
-
-        def wait_drain(step=step):
-            pltpu.make_async_remote_copy(
-                src_ref=drain.at[0],
-                dst_ref=drains.at[:, 2 - step],
-                send_sem=drain_sent.at[step + 2, 0],
-                recv_sem=drain_got.at[2 - step],
-                device_id=(w, n),
-                device_id_type=MESH,
-            ).wait_recv()
-
-        if step == 0:
-            pl.when(jnp.logical_not(bottom))(wait_drain)
-        else:
-            wait_drain()
+        needed = exists(-step) & jnp.logical_not(bottom) if step == 0 else exists(-step)
+        pl.when(needed)(drain_copy(step, 0).wait_recv)
 
     lane24 = iota((24, 128), 1)
     line = iota((24, 128), 0) + 4 * w - 8
-    inside = jnp.where((line >= 0) & (line < 4 * wide_count), 1.0, 0.0)
+    real = (line >= 0) & (line < 4 * wide_count)
+    inside = jnp.where(real, 1.0, 0.0)
     after_open = jnp.where(n < narrow_count - 1, 1.0, 0.0)
     before_open = jnp.where(n > 0, 1.0, 0.0)
     inside_halo = inside * jnp.where(lane24 < 64, after_open, before_open)
 
     def stacked(ref, a):
-        return jnp.concatenate([ref[a, s] for s in range(6)], axis=0)
-
-    heads = [[stacked(patches, 3 * l + t) * inside for t in range(3)] for l in range(3)]
+        return jnp.where(real, jnp.concatenate([ref[a, s] for s in range(6)], axis=0), 0.0)
+
+    heads = [[stacked(patches, 3 * l + t) for t in range(3)] for l in range(3)]
     flows = [stacked(drains, t) for t in range(3)]
     for l in range(3):
-        trans = [stacked(patches, 9 + 3 * l + t) * inside for t in range(3)]
+        trans = [stacked(patches, 9 + 3 * l + t) for t in range(3)]
         wests, easts = ring_left(trans, lane24), ring_right(trans, lane24)
         for t in range(3):
             centre = trans[t]
@@ -494,38 +461,18 @@
     aquifer_out = pltpu.make_async_copy(aquifer_part, aquifer_next, store_done.at[3])
     aquifer_out.start()
 
-    def answer_plane(z, carry):
-        rows_from(0, PEERS, rows_sent.at[0], rows_got.at[z]).wait_recv()
-        return send_plane(z, carry)
-
-    def await_plane(z, carry):
-        rows_from(0, PEERS, rows_sent.at[0], rows_got.at[z]).wait_recv()
-        return carry
-
-    lax.fori_loop(my_z + 1, depth, answer_plane, 0)
-    rows_from(0, PEERS - 1, rows_sent.at[0], rows_got.at[my_z]).wait_recv()
+    pl.when(my_z < depth // 2)(answer)
+    rows_from(PEERS - 1, my_z).wait_recv()
     lax.fori_loop(0, my_z, await_plane, 0)
 
     for copy in (rest_out, own_rows, part_out, aquifer_out):
         copy.wait()
-    for copy in patch_copies + face_copies + slab_copies:
+    for copy in slab_copies:
         copy.wait_send()
-    rows_from(0, wide_count - 1, rows_sent.at[0], rows_got.at[0]).wait_send()
-
-    @pl.when(bottom)
-    def _():
-        for step in (0, 1, -1, 2, -2):
-            for q in range(4):
-                if step == 0 and q == 3:
-                    continue
-                pltpu.make_async_remote_copy(
-                    src_ref=drain.at[q],
-                    dst_ref=drains.at[:, 2 - step],
-                    send_sem=drain_sent.at[step + 2, q],
-                    recv_sem=drain_got.at[2 - step],
-                    device_id=(w, n),
-                    device_id_type=MESH,
-                ).wait_send()
+    for copy, step in zip(patch_copies + face_copies, around + (1, -1)):
+        pl.when(exists(step))(copy.wait_send)
+    each_drain(lambda copy: copy.wait_send())
+    rows_from(wide_count - 1, 0).wait_send()
 
 
 def finish(
@@ -558,27 +505,28 @@
         ],
         axis=1,
     )
-    for k in range(CAP):
-        hit = rows == slot_lines[32 * k + 16 : 32 * k + 17, :]
-
-        def place(z, carry, k=k, hit=hit):
-            value = slot_lines[pl.ds(32 * k + z, 1), :]
-            value = jnp.where(hit, jnp.broadcast_to(value, (32, 128)), 0.0)
-            high = value.astype(BF16)
-            low = (value - high.astype(F32)).astype(BF16)
-            spread[pl.ds(pl.multiple_of(z * 32, 32), 32), 128 * k : 128 * k + 128] = high
-            spread[pl.ds(pl.multiple_of(z * 32 + 512, 32), 32), 128 * k : 128 * k + 128] = low
-            return carry
-
-        lax.fori_loop(0, 16, place, 0, unroll=4)
-    taken = lax.dot_general(spread[...], target, NT, preferred_element_type=F32)
+    hits = [rows == slot_lines[32 * k + 16 : 32 * k + 17, :] for k in range(CAP)]
     loads[1].wait()
     loads[2].wait()
-    out[...] = part[...] - (taken[:512] + taken[512:]) * rest[...]
-    stored = pltpu.make_async_copy(out, out_hbm, done.at[4])
-    stored.start()
+    stores = []
+    for i in range(4):
+        for layer in range(4):
+            for k in range(CAP):
+                line = 32 * k + 4 * i + layer
+                value = jnp.broadcast_to(slot_lines[line : line + 1, :], (32, 128))
+                value = jnp.where(hits[k], value, 0.0)
+                high = value.astype(BF16)
+                low = (value - high.astype(F32)).astype(BF16)
+                spread[i, 32 * layer : 32 * layer + 32, 128 * k : 128 * k + 128] = high
+                spread[i, 32 * layer + 128 : 32 * layer + 160, 128 * k : 128 * k + 128] = low
+        taken = lax.dot_general(spread[i], target, NT, preferred_element_type=F32)
+        at = pl.ds(128 * i, 128)
+        out[at, :] = part[at, :] - (taken[:128] + taken[128:]) * rest[at, :]
+        stores.append(pltpu.make_async_copy(out.at[at], out_hbm.at[at], done.at[4 + i]))
+        stores[i].start()
     loads[3].wait()
-    stored.wait()
+    for store in stores:
+        store.wait()
 
 
 def rows_of(a):
@@ -684,9 +632,9 @@
             pltpu.VMEM((512, 128), F32),
             pltpu.VMEM((512, 128), F32),
             pltpu.VMEM((512, 128), F32),
-            pltpu.VMEM((1024, 512), BF16),
+            pltpu.VMEM((4, 256, 512), BF16),
             pltpu.VMEM((128, 128), F32),
-            dma((5,)),
+            dma((8,)),
         ],
         compiler_params=pltpu.CompilerParams(vmem_limit_bytes=60 * 1024 * 1024),
         name="finish_step",

time: 35.4 us -> 30.3 us (0.86)
  the two profiles are of different devices: /device:TPU:1 before, /device:TPU:481 now
where the time goes in v6:
time: 30.3 us; the launch traced here: 30.1 us
  Pallas kernels  29.5 us (97%)
  between operations  0.64 us (2%)
    pallas_call x1, Pallas kernels, body(): pl.pallas_call(functools.partial(kernel, wide_count, narrow_count), out_s...  27.2 us
    pallas_call x1, Pallas kernels, body(): pl.pallas_call(finish, out_shape=(jax.ShapeDtypeStruct((512, 128), F32),...  2.25 us

profile of v6, /device:TPU:481, one launch (start us, length us, event | category | flops | bytes accessed | tf_op | source)
XLA Modules:
  0.0 30.1 jit_solution(13986314087932962152)
XLA Ops:
  0.6 27.2 %coupled_step.1 = (f32[128,1,128]{2,1,0:T(1,128)}, f32[512,128]{1,0:T(8,128)}, f32[512,128]{1,0:T(8,128)}, f32[24,128]{1,0:T(8,128)}) custom-call(f32[512,128]{1,0:T(8,128)} %bitcast.37, s32[512,128]{1,0:T(8,128)} %bitcast.38, f32[1,12]{1,0:T(1,128)} %bitcast.45, f32[1,12]{1,0:T(1,128)} %bitcast.46, f32[1,12]{1,0:T(1,128)} %bitcast.47, f32[16,256]{1,0:T(8,128)} %bitcast.42, ...), custom_call_target="tpu_custom_call" | custom-call | tf_op jit(solution)/shard_map/coupled_step/pallas_call | solution.py:558
  27.9 2.3 %finish_step.1 = (f32[512,128]{1,0:T(8,128)}, f32[24,128]{1,0:T(8,128)}) custom-call(f32[128,128]{1,0:T(8,128)} %bitcast.39, f32[512,128]{1,0:T(8,128)} %get-tuple-element.9.part_hbm, f32[512,128]{1,0:T(8,128)} %get-tuple-element.10.rest_hbm, f32[24,128]{1,0:T(8,128)} %get-tuple-element.11.aquifer_hbm), custom_call_target="tpu_custom_call" | custom-call | tf_op jit(solution)/shard_map/finish_step/pallas_call | solution.py:622

commit v7 on v6

--- a/solution.py
+++ b/solution.py
@@ -113,6 +113,9 @@
     face_in,
     slab_in,
     slots,
+    by_peer,
+    plane_rows,
+    by_plane,
     patch,
     patches,
     drain,
@@ -123,6 +126,9 @@
     load_done,
     rows_sent,
     rows_got,
+    answers_sent,
+    plane_sent,
+    plane_got,
     patch_sent,
     patch_got,
     drain_sent,
@@ -149,12 +155,20 @@
 
     peers = [(my_peer + j) % PEERS for j in range(1, PEERS + 1)]
 
-    def greet_plane(z, carry):
-        for peer in peers:
-            greet(z * PEERS + peer, n)
+    def plane_at(k):
+        return (my_z + depth // 2 + ((k + 1) // 2) * (1 - 2 * (k % 2)) + depth) % depth
+
+    def greet_plane(k, carry):
+        z = plane_at(k)
+
+        @pl.when(z > my_z)
+        def _():
+            for peer in peers:
+                greet(z * PEERS + peer, n)
+
         return carry
 
-    lax.fori_loop(my_z + 1, depth, greet_plane, 0)
+    lax.fori_loop(0, depth - 1, greet_plane, 0)
     for peer in peers[:-1]:
         greet(my_z * PEERS + peer, n)
     greeted = PEERS * my_z + PEERS - 1 + 2
@@ -192,6 +206,9 @@
         column_ref[...],
     )
     slots[...] = made
+    for z in range(depth):
+        for p in range(PEERS):
+            by_peer[p, z : z + 1] = slots[z * PEERS + p : z * PEERS + p + 1]
 
     for i in (8, 9):
         loads[i].wait()
@@ -257,27 +274,47 @@
 
     def send_rows(tile):
         remote(
-            slots.at[pl.ds(tile, 1)], rows.at[w], rows_sent.at[0], rows_got.at[my_z], tile, n
+            slots.at[pl.ds(tile, 1)], rows.at[pl.ds(w, 1)], rows_sent.at[0], rows_got.at[my_z], tile, n
         ).start()
 
     def rows_from(count, z):
         at = rows.at[pl.ds(0, count)]
         return remote(at, at, rows_sent.at[0], rows_got.at[z], w, n)
 
-    def send_plane(z, carry):
-        for peer in peers:
-            send_rows(z * PEERS + peer)
+    def send_plane(k, carry):
+        z = plane_at(k)
+
+        @pl.when(z < my_z)
+        def _():
+            for peer in peers:
+                send_rows(z * PEERS + peer)
+
         return carry
 
-    lax.fori_loop(0, my_z, send_plane, 0)
-    for peer in peers[:-1]:
-        send_rows(my_z * PEERS + peer)
-    own_rows = pltpu.make_async_copy(slots.at[pl.ds(w, 1)], rows.at[w], store_done.at[1])
-    own_rows.start()
+    lax.fori_loop(0, depth - 1, send_plane, 0)
+
+    plane_copies = [
+        remote(
+            by_peer.at[peer],
+            plane_rows.at[my_peer],
+            plane_sent.at[j],
+            plane_got.at[j],
+            my_z * PEERS + peer,
+            n,
+        )
+        for j, peer in enumerate(peers[:-1])
+    ]
+    for copy in plane_copies:
+        copy.start()
+
+    def rows_to(z):
+        return (by_plane.at[z], rows.at[pl.ds(my_z * PEERS, PEERS)])
 
     def answer_plane(z, carry):
         rows_from(PEERS, z).wait_recv()
-        return send_plane(z, carry)
+        to = z * PEERS + my_peer
+        remote(*rows_to(z), answers_sent.at[0], rows_got.at[my_z], to, n).start()
+        return carry
 
     def await_plane(z, carry):
         rows_from(PEERS, z).wait_recv()
@@ -332,6 +369,17 @@
     def answer():
         lax.fori_loop(my_z + 1, depth, answer_plane, 0)
 
+    def regroup():
+        for copy in plane_copies:
+            copy.wait_recv()
+        plane_rows[my_peer] = by_peer[my_peer]
+        for z in range(depth):
+            for p in range(PEERS):
+                by_plane[z, p : p + 1] = plane_rows[p, z : z + 1]
+        own = pltpu.make_async_copy(*rows_to(my_z), store_done.at[1])
+        own.start()
+        return own
+
     row = iota((32, 128), 0)
     lane = iota((32, 128), 1)
     across_open = jnp.where(row % 4 == 0, 0.0, 0.5)
@@ -365,7 +413,8 @@
     head, cond = layer(15)
     part[480:512, :] = head + (vertical_in + sides(head, cond)) * rest[480:512, :]
 
-    pl.when(my_z >= depth // 2)(answer)
+    own_rows = regroup()
+    pl.when(my_z >= depth // 4)(answer)
 
     for copy in slab_copies:
         copy.wait_recv()
@@ -461,8 +510,7 @@
     aquifer_out = pltpu.make_async_copy(aquifer_part, aquifer_next, store_done.at[3])
     aquifer_out.start()
 
-    pl.when(my_z < depth // 2)(answer)
-    rows_from(PEERS - 1, my_z).wait_recv()
+    pl.when(my_z < depth // 4)(answer)
     lax.fori_loop(0, my_z, await_plane, 0)
 
     for copy in (rest_out, own_rows, part_out, aquifer_out):
@@ -472,7 +520,19 @@
     for copy, step in zip(patch_copies + face_copies, around + (1, -1)):
         pl.when(exists(step))(copy.wait_send)
     each_drain(lambda copy: copy.wait_send())
-    rows_from(wide_count - 1, 0).wait_send()
+    for copy in plane_copies:
+        copy.wait_send()
+
+    def left_plane(z, carry):
+        rows_from(PEERS, 0).wait_send()
+        return carry
+
+    def left_answer(z, carry):
+        remote(*rows_to(0), answers_sent.at[0], rows_got.at[0], w, n).wait_send()
+        return carry
+
+    lax.fori_loop(0, my_z, left_plane, 0)
+    lax.fori_loop(my_z + 1, depth, left_answer, 0)
 
 
 def finish(
@@ -558,7 +618,7 @@
     rows_in, part, rest, aquifer_next = pl.pallas_call(
         functools.partial(kernel, wide_count, narrow_count),
         out_shape=(
-            jax.ShapeDtypeStruct((wide_count, 1, 128), F32),
+            jax.ShapeDtypeStruct((wide_count, 128), F32),
             jax.ShapeDtypeStruct((512, 128), F32),
             jax.ShapeDtypeStruct((512, 128), F32),
             jax.ShapeDtypeStruct((24, 128), F32),
@@ -584,6 +644,9 @@
             pltpu.VMEM((2, 2, 128, 128), F32),
             pltpu.VMEM((2, 2, 32, 128), F32),
             pltpu.VMEM((wide_count, 128), F32),
+            pltpu.VMEM((PEERS, depth, 128), F32),
+            pltpu.VMEM((PEERS, depth, 128), F32),
+            pltpu.VMEM((depth, PEERS, 128), F32),
             pltpu.VMEM((18, 4, 128), F32),
             pltpu.VMEM((18, 6, 4, 128), F32),
             pltpu.VMEM((4, 3, 4, 128), F32),
@@ -594,6 +657,9 @@
             dma((10,)),
             dma((1,)),
             dma((depth,)),
+            dma((1,)),
+            dma((PEERS - 1,)),
+            dma((PEERS - 1,)),
             dma((4,)),
             dma((4,)),
             dma((5, 4)),
@@ -638,7 +704,7 @@
         ],
         compiler_params=pltpu.CompilerParams(vmem_limit_bytes=60 * 1024 * 1024),
         name="finish_step",
-    )(rows_in.reshape(128, 128), part, rest, aquifer_next)
+    )(rows_in, part, rest, aquifer_next)
     return grid_of(out, 16, 1024), grid_of(aquifer_out, 3, 256)
 
 

time: 30.3 us -> 28.1 us (0.927)
  the two profiles are of different devices: /device:TPU:481 before, /device:TPU:1 now
where the time goes in v7:
time: 28.1 us; the launch traced here: 28 us
  Pallas kernels  27.3 us (97%)
  between operations  0.64 us (2%)
    pallas_call x1, Pallas kernels, body(): pl.pallas_call(functools.partial(kernel, wide_count, narrow_count), out_s...  25.1 us
    pallas_call x1, Pallas kernels, body(): pl.pallas_call(finish, out_shape=(jax.ShapeDtypeStruct((512, 128), F32),...  2.25 us

profile of v7, /device:TPU:1, one launch (start us, length us, event | category | flops | bytes accessed | tf_op | source)
XLA Modules:
  0.0 28.0 jit_solution(17303626015229942077)
XLA Ops:
  0.6 25.1 %coupled_step.1 = (f32[128,128]{1,0:T(8,128)}, f32[512,128]{1,0:T(8,128)}, f32[512,128]{1,0:T(8,128)}, f32[24,128]{1,0:T(8,128)}) custom-call(f32[512,128]{1,0:T(8,128)} %bitcast.36, s32[512,128]{1,0:T(8,128)} %bitcast.37, f32[1,12]{1,0:T(1,128)} %bitcast.43, f32[1,12]{1,0:T(1,128)} %bitcast.44, f32[1,12]{1,0:T(1,128)} %bitcast.45, f32[16,256]{1,0:T(8,128)} %bitcast.40, ...), custom_call_target="tpu_custom_call" | custom-call | tf_op jit(solution)/shard_map/coupled_step/pallas_call | solution.py:618
  25.7 2.2 %finish_step.1 = (f32[512,128]{1,0:T(8,128)}, f32[24,128]{1,0:T(8,128)}) custom-call(f32[128,128]{1,0:T(8,128)} %get-tuple-element.8.rows_hbm, f32[512,128]{1,0:T(8,128)} %get-tuple-element.9.part_hbm, f32[512,128]{1,0:T(8,128)} %get-tuple-element.10.rest_hbm, f32[24,128]{1,0:T(8,128)} %get-tuple-element.11.aquifer_hbm), custom_call_target="tpu_custom_call" | custom-call | tf_op jit(solution)/shard_map/finish_step/pallas_call | solution.py:688

commit v8 on v7

--- a/solution.py
+++ b/solution.py
@@ -13,6 +13,7 @@
 LEAKANCE = 0.5
 PEERS = 8
 CAP = 4
+VMEM_GRANT = 32 * 1024 * 1024
 F32, BF16, I32 = jnp.float32, jnp.bfloat16, jnp.int32
 MESH = pl.DeviceIdType.MESH
 NT = (((1,), (1,)), ((), ()))
@@ -92,8 +93,8 @@
     aquifer_hbm,
     trans_hbm,
     rows,
-    part_hbm,
-    rest_hbm,
+    part,
+    rest,
     aquifer_next,
     head_ref,
     texture_ref,
@@ -107,8 +108,6 @@
     trans_ref,
     table,
     soil,
-    rest,
-    part,
     face_out,
     face_in,
     slab_in,
@@ -121,8 +120,6 @@
     drain,
     drains,
     coef,
-    aquifer_part,
-    store_done,
     load_done,
     rows_sent,
     rows_got,
@@ -210,6 +207,58 @@
         for p in range(PEERS):
             by_peer[p, z : z + 1] = slots[z * PEERS + p : z * PEERS + p + 1]
 
+    near_tiles = sum(jnp.where(exists(step), 1, 0) for step in (-2, -1, 0, 1, 2))
+    greeted = greeted + jnp.where(bottom, (narrow_count - 1) * near_tiles, 0)
+    pl.semaphore_wait(barrier, greeted)
+
+    def send_rows(tile):
+        remote(
+            slots.at[pl.ds(tile, 1)], rows.at[pl.ds(w, 1)], rows_sent.at[0], rows_got.at[my_z], tile, n
+        ).start()
+
+    def rows_from(count, z):
+        at = rows.at[pl.ds(0, count)]
+        return remote(at, at, rows_sent.at[0], rows_got.at[z], w, n)
+
+    def send_plane(k, carry):
+        z = plane_at(k)
+
+        @pl.when(z < my_z)
+        def _():
+            for peer in peers:
+                send_rows(z * PEERS + peer)
+
+        return carry
+
+    lax.fori_loop(0, depth - 1, send_plane, 0)
+
+    plane_copies = [
+        remote(
+            by_peer.at[peer],
+            plane_rows.at[my_peer],
+            plane_sent.at[j],
+            plane_got.at[j],
+            my_z * PEERS + peer,
+            n,
+        )
+        for j, peer in enumerate(peers[:-1])
+    ]
+    for copy in plane_copies:
+        copy.start()
+
+    def rows_to(z):
+        return (by_plane.at[z], rows.at[pl.ds(my_z * PEERS, PEERS)])
+
+    def answer_plane(z, carry):
+        rows_from(PEERS, z).wait_recv()
+        to = z * PEERS + my_peer
+        remote(*rows_to(z), answers_sent.at[0], rows_got.at[my_z], to, n).start()
+        return carry
+
+    def await_plane(z, carry):
+        rows_from(PEERS, z).wait_recv()
+        return carry
+
     for i in (8, 9):
         loads[i].wait()
     lane4 = iota((4, 128), 1)
@@ -251,8 +300,6 @@
         return carry
 
     lax.fori_loop(0, 16, conduct_layer, 0, unroll=4)
-    rest_out = pltpu.make_async_copy(rest, rest_hbm, store_done.at[0])
-    rest_out.start()
 
     for i, first in ((0, 3), (1, 0)):
         for v in range(2):
@@ -267,58 +314,6 @@
             before = flow[8 * q - 4 : 8 * q] if q > 0 else jnp.zeros((4, 128), F32)
             drain[q, 2] = jnp.where(lane4 < 64, after, before)
         drains[:, 2] = drain[3]
-
-    near_tiles = sum(jnp.where(exists(step), 1, 0) for step in (-2, -1, 0, 1, 2))
-    greeted = greeted + jnp.where(bottom, (narrow_count - 1) * near_tiles, 0)
-    pl.semaphore_wait(barrier, greeted)
-
-    def send_rows(tile):
-        remote(
-            slots.at[pl.ds(tile, 1)], rows.at[pl.ds(w, 1)], rows_sent.at[0], rows_got.at[my_z], tile, n
-        ).start()
-
-    def rows_from(count, z):
-        at = rows.at[pl.ds(0, count)]
-        return remote(at, at, rows_sent.at[0], rows_got.at[z], w, n)
-
-    def send_plane(k, carry):
-        z = plane_at(k)
-
-        @pl.when(z < my_z)
-        def _():
-            for peer in peers:
-                send_rows(z * PEERS + peer)
-
-        return carry
-
-    lax.fori_loop(0, depth - 1, send_plane, 0)
-
-    plane_copies = [
-        remote(
-            by_peer.at[peer],
-            plane_rows.at[my_peer],
-            plane_sent.at[j],
-            plane_got.at[j],
-            my_z * PEERS + peer,
-            n,
-        )
-        for j, peer in enumerate(peers[:-1])
-    ]
-    for copy in plane_copies:
-        copy.start()
-
-    def rows_to(z):
-        return (by_plane.at[z], rows.at[pl.ds(my_z * PEERS, PEERS)])
-
-    def answer_plane(z, carry):
-        rows_from(PEERS, z).wait_recv()
-        to = z * PEERS + my_peer
-        remote(*rows_to(z), answers_sent.at[0], rows_got.at[my_z], to, n).start()
-        return carry
-
-    def await_plane(z, carry):
-        rows_from(PEERS, z).wait_recv()
-        return carry
 
     face_copies = [
         remote(face_out.at[i], face_in.at[i], face_sent.at[i], face_got.at[i], w + step, n)
@@ -376,9 +371,7 @@
         for z in range(depth):
             for p in range(PEERS):
                 by_plane[z, p : p + 1] = plane_rows[p, z : z + 1]
-        own = pltpu.make_async_copy(*rows_to(my_z), store_done.at[1])
-        own.start()
-        return own
+        rows[pl.ds(pl.multiple_of(my_z * PEERS, PEERS), PEERS), :] = by_plane[my_z]
 
     row = iota((32, 128), 0)
     lane = iota((32, 128), 1)
@@ -413,7 +406,7 @@
     head, cond = layer(15)
     part[480:512, :] = head + (vertical_in + sides(head, cond)) * rest[480:512, :]
 
-    own_rows = regroup()
+    regroup()
     pl.when(my_z >= depth // 4)(answer)
 
     for copy in slab_copies:
@@ -435,8 +428,6 @@
         at = pl.ds(first, 128, stride=4)
         flow = jnp.where(is_open, factor * (cond + other_cond) * jump, 0.0)
         part[at, :] = part[at, :] + flow * rest[at, :]
-    part_out = pltpu.make_async_copy(part, part_hbm, store_done.at[2])
-    part_out.start()
 
     for copy, step in zip(patch_copies, around):
         pl.when(exists(-step))(copy.wait_recv)
@@ -504,17 +495,13 @@
 
     flat = lax.fori_loop(0, SWEEPS, sweep, tuple(v for layer in heads for v in layer))
     for l in range(3):
-        aquifer_part[8 * l : 8 * l + 8, :] = jnp.concatenate(
+        aquifer_next[8 * l : 8 * l + 8, :] = jnp.concatenate(
             [flat[3 * l][8:12], flat[3 * l + 1][8:12]], axis=0
         )
-    aquifer_out = pltpu.make_async_copy(aquifer_part, aquifer_next, store_done.at[3])
-    aquifer_out.start()
 
     pl.when(my_z < depth // 4)(answer)
     lax.fori_loop(0, my_z, await_plane, 0)
 
-    for copy in (rest_out, own_rows, part_out, aquifer_out):
-        copy.wait()
     for copy in slab_copies:
         copy.wait_send()
     for copy, step in zip(patch_copies + face_copies, around + (1, -1)):
@@ -536,25 +523,19 @@
 
 
 def finish(
-    rows_hbm,
-    part_hbm,
-    rest_hbm,
-    aquifer_hbm,
-    out_hbm,
-    aquifer_out_hbm,
     rows_in,
     part,
     rest,
+    aquifer_next,
+    out_hbm,
+    aquifer_out_hbm,
     out,
     spread,
     slot_lines,
     done,
 ):
-    pairs = ((rows_hbm, rows_in), (part_hbm, part), (rest_hbm, rest), (aquifer_hbm, aquifer_out_hbm))
-    loads = [pltpu.make_async_copy(a, b, done.at[i]) for i, (a, b) in enumerate(pairs)]
-    for load in loads:
-        load.start()
-    loads[0].wait()
+    aquifer_out = pltpu.make_async_copy(aquifer_next, aquifer_out_hbm, done.at[4])
+    aquifer_out.start()
     slot_lines[...] = rows_in[...].T
     lanes = iota((128, 128), 0).astype(F32)
     rows = iota((32, 128), 0).astype(F32)
@@ -566,8 +547,6 @@
         axis=1,
     )
     hits = [rows == slot_lines[32 * k + 16 : 32 * k + 17, :] for k in range(CAP)]
-    loads[1].wait()
-    loads[2].wait()
     stores = []
     for i in range(4):
         for layer in range(4):
@@ -582,9 +561,9 @@
         taken = lax.dot_general(spread[i], target, NT, preferred_element_type=F32)
         at = pl.ds(128 * i, 128)
         out[at, :] = part[at, :] - (taken[:128] + taken[128:]) * rest[at, :]
-        stores.append(pltpu.make_async_copy(out.at[at], out_hbm.at[at], done.at[4 + i]))
+        stores.append(pltpu.make_async_copy(out.at[at], out_hbm.at[at], done.at[i]))
         stores[i].start()
-    loads[3].wait()
+    aquifer_out.wait()
     for store in stores:
         store.wait()
 
@@ -614,17 +593,17 @@
     narrow_count = lax.axis_size("narrow")
     depth = wide_count // PEERS
     dma = pltpu.SemaphoreType.DMA
-    hbm = pl.BlockSpec(memory_space=pl.ANY)
+    hbm, vmem = pl.BlockSpec(memory_space=pltpu.HBM), pl.BlockSpec(memory_space=pltpu.VMEM)
     rows_in, part, rest, aquifer_next = pl.pallas_call(
         functools.partial(kernel, wide_count, narrow_count),
         out_shape=(
-            jax.ShapeDtypeStruct((wide_count, 128), F32),
-            jax.ShapeDtypeStruct((512, 128), F32),
-            jax.ShapeDtypeStruct((512, 128), F32),
-            jax.ShapeDtypeStruct((24, 128), F32),
+            pltpu.VMEM((wide_count, 128), F32),
+            pltpu.VMEM((512, 128), F32),
+            pltpu.VMEM((512, 128), F32),
+            pltpu.VMEM((24, 128), F32),
         ),
         in_specs=[hbm] * 10,
-        out_specs=[hbm] * 4,
+        out_specs=[vmem] * 4,
         scratch_shapes=[
             pltpu.VMEM((512, 128), F32),
             pltpu.VMEM((512, 128), I32),
@@ -638,8 +617,6 @@
             pltpu.VMEM((96, 128), F32),
             pltpu.VMEM((24, 128), F32),
             pltpu.VMEM((2, 512, 128), F32),
-            pltpu.VMEM((512, 128), F32),
-            pltpu.VMEM((512, 128), F32),
             pltpu.VMEM((2, 2, 128, 128), F32),
             pltpu.VMEM((2, 2, 128, 128), F32),
             pltpu.VMEM((2, 2, 32, 128), F32),
@@ -652,8 +629,6 @@
             pltpu.VMEM((4, 3, 4, 128), F32),
             pltpu.VMEM((3, 6, 4, 128), F32),
             pltpu.VMEM((6, 9, 24, 128), F32),
-            pltpu.VMEM((24, 128), F32),
-            dma((4,)),
             dma((10,)),
             dma((1,)),
             dma((depth,)),
@@ -670,20 +645,25 @@
             dma((2,)),
         ],
         compiler_params=pltpu.CompilerParams(
-            collective_id=0, has_side_effects=True, vmem_limit_bytes=60 * 1024 * 1024
+            collective_id=0, has_side_effects=True, vmem_limit_bytes=VMEM_GRANT
         ),
         name="coupled_step",
     )(
-        rows_of(pressure_head),
-        rows_of(texture),
-        saturated_table.reshape(1, -1),
-        shape_table.reshape(1, -1),
-        capacity_table.reshape(1, -1),
-        uptake.T,
-        root_tile.reshape(1, -1),
-        root_column.reshape(1, -1),
-        rows_of(aquifer_head),
-        rows_of(transmissivity),
+        *(
+            pltpu.with_memory_space_constraint(a, pltpu.HBM)
+            for a in (
+                rows_of(pressure_head),
+                rows_of(texture),
+                saturated_table.reshape(1, -1),
+                shape_table.reshape(1, -1),
+                capacity_table.reshape(1, -1),
+                uptake.T,
+                root_tile.reshape(1, -1),
+                root_column.reshape(1, -1),
+                rows_of(aquifer_head),
+                rows_of(transmissivity),
+            )
+        )
     )
     out, aquifer_out = pl.pallas_call(
         finish,
@@ -691,18 +671,15 @@
             jax.ShapeDtypeStruct((512, 128), F32),
             jax.ShapeDtypeStruct((24, 128), F32),
         ),
-        in_specs=[hbm] * 4,
+        in_specs=[vmem] * 4,
         out_specs=[hbm] * 2,
         scratch_shapes=[
-            pltpu.VMEM((128, 128), F32),
-            pltpu.VMEM((512, 128), F32),
-            pltpu.VMEM((512, 128), F32),
             pltpu.VMEM((512, 128), F32),
             pltpu.VMEM((4, 256, 512), BF16),
             pltpu.VMEM((128, 128), F32),
-            dma((8,)),
+            dma((5,)),
         ],
-        compiler_params=pltpu.CompilerParams(vmem_limit_bytes=60 * 1024 * 1024),
+        compiler_params=pltpu.CompilerParams(vmem_limit_bytes=VMEM_GRANT),
         name="finish_step",
     )(rows_in, part, rest, aquifer_next)
     return grid_of(out, 16, 1024), grid_of(aquifer_out, 3, 256)

time: 28.1 us -> 27 us (0.961)
  Pallas kernels: 27.3 us -> 26.2 us
    pallas_call x1, Pallas kernels: 2.25 us -> 1.28 us  [body(): pl.pallas_call(finish, out_shape=(jax.ShapeDtypeStruct((512, 128), F32),...]
where the time goes in v8:
time: 27 us; the launch traced here: 26.9 us
  Pallas kernels  26.2 us (97%)
  between operations  0.64 us (2%)
    pallas_call x1, Pallas kernels, body(): pl.pallas_call(functools.partial(kernel, wide_count, narrow_count), out_s...  24.9 us
    pallas_call x1, Pallas kernels, body(): pl.pallas_call(finish, out_shape=(jax.ShapeDtypeStruct((512, 128), F32),...  1.28 us

profile of v8, /device:TPU:1, one launch (start us, length us, event | category | flops | bytes accessed | tf_op | source)
XLA Modules:
  0.0 26.9 jit_solution(5088729162740969105)
XLA Ops:
  0.6 24.9 %coupled_step.1 = (f32[128,128]{1,0:T(8,128)S(1)}, f32[512,128]{1,0:T(8,128)S(1)}, f32[512,128]{1,0:T(8,128)S(1)}, f32[24,128]{1,0:T(8,128)S(1)}) custom-call(f32[512,128]{1,0:T(8,128)} %bitcast.36, s32[512,128]{1,0:T(8,128)} %bitcast.37, f32[1,12]{1,0:T(1,128)} %bitcast.43, f32[1,12]{1,0:T(1,128)} %bitcast.44, f32[1,12]{1,0:T(1,128)} %bitcast.45, ...), custom_call_target="tpu_custom_call" | custom-call | tf_op jit(solution)/shard_map/coupled_step/pallas_call | solution.py:597
  25.6 1.3 %finish_step.1 = (f32[512,128]{1,0:T(8,128)}, f32[24,128]{1,0:T(8,128)}) custom-call(f32[128,128]{1,0:T(8,128)S(1)} %get-tuple-element.8.rows_in, f32[512,128]{1,0:T(8,128)S(1)} %get-tuple-element.9.part, f32[512,128]{1,0:T(8,128)S(1)} %get-tuple-element.10.rest, f32[24,128]{1,0:T(8,128)S(1)} %get-tuple-element.11.aquifer_next), custom_call_target="tpu_custom_call" | custom-call | tf_op jit(solution)/shard_map/finish_step/pallas_call | solution.py:668

commit v9 on v8

--- a/solution.py
+++ b/solution.py
@@ -92,9 +92,7 @@
     column_hbm,
     aquifer_hbm,
     trans_hbm,
-    rows,
-    part,
-    rest,
+    out,
     aquifer_next,
     head_ref,
     texture_ref,
@@ -108,6 +106,11 @@
     trans_ref,
     table,
     soil,
+    rows,
+    part,
+    rest,
+    spread,
+    slot_lines,
     face_out,
     face_in,
     slab_in,
@@ -165,7 +168,6 @@
 
         return carry
 
-    lax.fori_loop(0, depth - 1, greet_plane, 0)
     for peer in peers[:-1]:
         greet(my_z * PEERS + peer, n)
     greeted = PEERS * my_z + PEERS - 1 + 2
@@ -185,6 +187,8 @@
         @pl.when(jnp.logical_not(bottom) & exists(step))
         def _(step=step):
             greet(w + step, narrow_count - 1)
+
+    lax.fori_loop(0, depth - 1, greet_plane, 0)
 
     order = (6, 7, 5, 0, 1, 2, 3, 4, 8, 9)
     held = (head_ref, texture_ref, saturated_ref, shape_ref, capacity_ref, uptake_ref, tile_ref)
@@ -361,8 +365,10 @@
 
     each_drain(lambda copy: copy.start())
 
-    def answer():
-        lax.fori_loop(my_z + 1, depth, answer_plane, 0)
+    half = depth // 2
+
+    def answer(low, high):
+        lax.fori_loop(jnp.maximum(my_z + 1, low), high, answer_plane, 0)
 
     def regroup():
         for copy in plane_copies:
@@ -407,7 +413,7 @@
     part[480:512, :] = head + (vertical_in + sides(head, cond)) * rest[480:512, :]
 
     regroup()
-    pl.when(my_z >= depth // 4)(answer)
+    pl.when(my_z >= depth // 4)(lambda: answer(0, depth))
 
     for copy in slab_copies:
         copy.wait_recv()
@@ -499,8 +505,43 @@
             [flat[3 * l][8:12], flat[3 * l + 1][8:12]], axis=0
         )
 
-    pl.when(my_z < depth // 4)(answer)
-    lax.fori_loop(0, my_z, await_plane, 0)
+    lanes = iota((128, 128), 0).astype(F32)
+    cell_rows = iota((32, 128), 0).astype(F32)
+
+    def scatter(which, result):
+        some = rows[pl.ds(pl.multiple_of(which * (wide_count // 2), 64), 64), :]
+        slot_lines[...] = jnp.concatenate([some, roll(some, 64, 1)], axis=0).T
+        pairs = range(CAP // 2)
+        target = jnp.concatenate(
+            [
+                (lanes == slot_lines[32 * k + 17 : 32 * k + 18, :]).astype(F32).astype(BF16)
+                for k in pairs
+            ],
+            axis=1,
+        )
+        hits = [cell_rows == slot_lines[32 * k + 16 : 32 * k + 17, :] for k in pairs]
+        for i in range(4):
+            for layer in range(4):
+                for k in pairs:
+                    line = 32 * k + 4 * i + layer
+                    value = jnp.broadcast_to(slot_lines[line : line + 1, :], (32, 128))
+                    value = jnp.where(hits[k], value, 0.0)
+                    high = value.astype(BF16)
+                    low = (value - high.astype(F32)).astype(BF16)
+                    at = pl.ds(128 * k, 128)
+                    spread[i, 32 * layer : 32 * layer + 32, at] = high
+                    spread[i, 32 * layer + 128 : 32 * layer + 160, at] = low
+            taken = lax.dot_general(spread[i], target, NT, preferred_element_type=F32)
+            at = pl.ds(128 * i, 128)
+            result[at, :] = part[at, :] - (taken[:128] + taken[128:]) * rest[at, :]
+
+    mine = my_z // half
+    pl.when(my_z < depth // 4)(lambda: answer(0, half))
+    lax.fori_loop(mine * half, my_z, await_plane, 0)
+    scatter(mine, part)
+    pl.when(my_z < depth // 4)(lambda: answer(half, depth))
+    lax.fori_loop(0, mine * half, await_plane, 0)
+    scatter(1 - mine, out)
 
     for copy in slab_copies:
         copy.wait_send()
@@ -522,50 +563,15 @@
     lax.fori_loop(my_z + 1, depth, left_answer, 0)
 
 
-def finish(
-    rows_in,
-    part,
-    rest,
-    aquifer_next,
-    out_hbm,
-    aquifer_out_hbm,
-    out,
-    spread,
-    slot_lines,
-    done,
-):
-    aquifer_out = pltpu.make_async_copy(aquifer_next, aquifer_out_hbm, done.at[4])
-    aquifer_out.start()
-    slot_lines[...] = rows_in[...].T
-    lanes = iota((128, 128), 0).astype(F32)
-    rows = iota((32, 128), 0).astype(F32)
-    target = jnp.concatenate(
-        [
-            (lanes == slot_lines[32 * k + 17 : 32 * k + 18, :]).astype(F32).astype(BF16)
-            for k in range(CAP)
-        ],
-        axis=1,
-    )
-    hits = [rows == slot_lines[32 * k + 16 : 32 * k + 17, :] for k in range(CAP)]
-    stores = []
+def store(head_next, aquifer_next, head_out, aquifer_out, done):
+    copies = [pltpu.make_async_copy(aquifer_next, aquifer_out, done.at[4])]
     for i in range(4):
-        for layer in range(4):
-            for k in range(CAP):
-                line = 32 * k + 4 * i + layer
-                value = jnp.broadcast_to(slot_lines[line : line + 1, :], (32, 128))
-                value = jnp.where(hits[k], value, 0.0)
-                high = value.astype(BF16)
-                low = (value - high.astype(F32)).astype(BF16)
-                spread[i, 32 * layer : 32 * layer + 32, 128 * k : 128 * k + 128] = high
-                spread[i, 32 * layer + 128 : 32 * layer + 160, 128 * k : 128 * k + 128] = low
-        taken = lax.dot_general(spread[i], target, NT, preferred_element_type=F32)
         at = pl.ds(128 * i, 128)
-        out[at, :] = part[at, :] - (taken[:128] + taken[128:]) * rest[at, :]
-        stores.append(pltpu.make_async_copy(out.at[at], out_hbm.at[at], done.at[i]))
-        stores[i].start()
-    aquifer_out.wait()
-    for store in stores:
-        store.wait()
+        copies.append(pltpu.make_async_copy(head_next.at[at], head_out.at[at], done.at[i]))
+    for copy in copies:
+        copy.start()
+    for copy in copies:
+        copy.wait()
 
 
 def rows_of(a):
@@ -594,16 +600,14 @@
     depth = wide_count // PEERS
     dma = pltpu.SemaphoreType.DMA
     hbm, vmem = pl.BlockSpec(memory_space=pltpu.HBM), pl.BlockSpec(memory_space=pltpu.VMEM)
-    rows_in, part, rest, aquifer_next = pl.pallas_call(
+    head_next, aquifer_next = pl.pallas_call(
         functools.partial(kernel, wide_count, narrow_count),
         out_shape=(
-            pltpu.VMEM((wide_count, 128), F32),
-            pltpu.VMEM((512, 128), F32),
             pltpu.VMEM((512, 128), F32),
             pltpu.VMEM((24, 128), F32),
         ),
         in_specs=[hbm] * 10,
-        out_specs=[vmem] * 4,
+        out_specs=[vmem] * 2,
         scratch_shapes=[
             pltpu.VMEM((512, 128), F32),
             pltpu.VMEM((512, 128), I32),
@@ -617,6 +621,11 @@
             pltpu.VMEM((96, 128), F32),
             pltpu.VMEM((24, 128), F32),
             pltpu.VMEM((2, 512, 128), F32),
+            pltpu.VMEM((wide_count, 128), F32),
+            pltpu.VMEM((512, 128), F32),
+            pltpu.VMEM((512, 128), F32),
+            pltpu.VMEM((4, 256, 256), BF16),
+            pltpu.VMEM((128, 128), F32),
             pltpu.VMEM((2, 2, 128, 128), F32),
             pltpu.VMEM((2, 2, 128, 128), F32),
             pltpu.VMEM((2, 2, 32, 128), F32),
@@ -666,22 +675,17 @@
         )
     )
     out, aquifer_out = pl.pallas_call(
-        finish,
+        store,
         out_shape=(
             jax.ShapeDtypeStruct((512, 128), F32),
             jax.ShapeDtypeStruct((24, 128), F32),
         ),
-        in_specs=[vmem] * 4,
+        in_specs=[vmem] * 2,
         out_specs=[hbm] * 2,
-        scratch_shapes=[
-            pltpu.VMEM((512, 128), F32),
-            pltpu.VMEM((4, 256, 512), BF16),
-            pltpu.VMEM((128, 128), F32),
-            dma((5,)),
-        ],
+        scratch_shapes=[dma((5,))],
         compiler_params=pltpu.CompilerParams(vmem_limit_bytes=VMEM_GRANT),
         name="finish_step",
-    )(rows_in, part, rest, aquifer_next)
+    )(head_next, aquifer_next)
     return grid_of(out, 16, 1024), grid_of(aquifer_out, 3, 256)
 
 

time: 27 us -> 26.4 us (0.978)
  Pallas kernels: 26.2 us -> 25.6 us
    pallas_call x1, Pallas kernels: 1.28 us -> 0.74 us  [body(): pl.pallas_call(store, out_shape=(jax.ShapeDtypeStruct((512, 128), F32), j...]
where the time goes in v9:
time: 26.4 us; the launch traced here: 26.2 us
  Pallas kernels  25.6 us (97%)
  between operations  0.64 us (2%)
    pallas_call x1, Pallas kernels, body(): pl.pallas_call(functools.partial(kernel, wide_count, narrow_count), out_s...  24.8 us
    pallas_call x1, Pallas kernels, body(): pl.pallas_call(store, out_shape=(jax.ShapeDtypeStruct((512, 128), F32), j...  0.74 us

profile of v9, /device:TPU:1, one launch (start us, length us, event | category | flops | bytes accessed | tf_op | source)
XLA Modules:
  0.0 26.2 jit_solution(10115405383061430181)
XLA Ops:
  0.6 24.8 %coupled_step.1 = (f32[512,128]{1,0:T(8,128)S(1)}, f32[24,128]{1,0:T(8,128)S(1)}) custom-call(f32[512,128]{1,0:T(8,128)} %bitcast.36, s32[512,128]{1,0:T(8,128)} %bitcast.37, f32[1,12]{1,0:T(1,128)} %bitcast.43, f32[1,12]{1,0:T(1,128)} %bitcast.44, f32[1,12]{1,0:T(1,128)} %bitcast.45, f32[16,256]{1,0:T(8,128)} %bitcast.40, s32[1,256]{1,0:T(1,128)} %bitcast.41, ...), custom_call_target="tpu_custom_call" | custom-call | tf_op jit(solution)/shard_map/coupled_step/pallas_call | solution.py:603
  25.5 0.7 %finish_step.1 = (f32[512,128]{1,0:T(8,128)}, f32[24,128]{1,0:T(8,128)}) custom-call(f32[512,128]{1,0:T(8,128)S(1)} %get-tuple-element.6.head_next, f32[24,128]{1,0:T(8,128)S(1)} %get-tuple-element.7.aquifer_next), custom_call_target="tpu_custom_call" | custom-call | tf_op jit(solution)/shard_map/finish_step/pallas_call | solution.py:677

commit v10 on v9

--- a/solution.py
+++ b/solution.py
@@ -229,8 +229,9 @@
 
         @pl.when(z < my_z)
         def _():
-            for peer in peers:
-                send_rows(z * PEERS + peer)
+            for core in (0, 1):
+                for j in range(1, PEERS // 2 + 1):
+                    send_rows(z * PEERS + (2 * (my_peer // 2) + 2 * j) % PEERS + core)
 
         return carry
 

time: 26.4 us -> 26.4 us (level)
  no operation moved by 1% of the time
where the time goes in v10:
time: 26.4 us; the launch traced here: 26.2 us
  Pallas kernels  25.6 us (97%)
  between operations  0.64 us (2%)
    pallas_call x1, Pallas kernels, body(): pl.pallas_call(functools.partial(kernel, wide_count, narrow_count), out_s...  24.9 us
    pallas_call x1, Pallas kernels, body(): pl.pallas_call(store, out_shape=(jax.ShapeDtypeStruct((512, 128), F32), j...  0.74 us

profile of v10, /device:TPU:1, one launch (start us, length us, event | category | flops | bytes accessed | tf_op | source)
XLA Modules:
  0.0 26.2 jit_solution(14595653256861342146)
XLA Ops:
  0.6 24.9 %coupled_step.1 = (f32[512,128]{1,0:T(8,128)S(1)}, f32[24,128]{1,0:T(8,128)S(1)}) custom-call(f32[512,128]{1,0:T(8,128)} %bitcast.36, s32[512,128]{1,0:T(8,128)} %bitcast.37, f32[1,12]{1,0:T(1,128)} %bitcast.43, f32[1,12]{1,0:T(1,128)} %bitcast.44, f32[1,12]{1,0:T(1,128)} %bitcast.45, f32[16,256]{1,0:T(8,128)} %bitcast.40, s32[1,256]{1,0:T(1,128)} %bitcast.41, ...), custom_call_target="tpu_custom_call" | custom-call | tf_op jit(solution)/shard_map/coupled_step/pallas_call | solution.py:604
  25.5 0.7 %finish_step.1 = (f32[512,128]{1,0:T(8,128)}, f32[24,128]{1,0:T(8,128)}) custom-call(f32[512,128]{1,0:T(8,128)S(1)} %get-tuple-element.6.head_next, f32[24,128]{1,0:T(8,128)S(1)} %get-tuple-element.7.aquifer_next), custom_call_target="tpu_custom_call" | custom-call | tf_op jit(solution)/shard_map/finish_step/pallas_call | solution.py:678
